TPU v7x, 32 devices: a whole 2x2x4 slice. The times are simulated.
32 devices in a mesh: ctx: 4 (over x, core), exp: 8 (over z, y).
Axes of the slice: x: 2, y: 2, z: 4, core: 2. Of those that a mesh axis runs over, the one named last changes fastest.
Arguments:
- hidden_in: bfloat16 [8, 512, 2048], P('exp', 'ctx'), may hold values from -6 to 6
- grad_out: bfloat16 [8, 512, 2048], P('exp', 'ctx'), may hold values from -6 to 6
- post_gain: float32 [2048], replicated, may hold values from 0.1 to 1.9
- route_ids: int32 [8, 512, 10], P('exp', 'ctx'), may hold values from 0 to 511, as said below
- route_weight: float32 [8, 512, 10], P('exp', 'ctx'), may hold values from 0.02 to 0.3
- gate_up: bfloat16 [32, 2048, 1024], P(('ctx', 'exp')), may hold values from -0.125 to 0.125
- down_proj: bfloat16 [32, 512, 2048], P(('ctx', 'exp')), may hold values from -0.25 to 0.25
- query_in: bfloat16 [8, 512, 1024], P('exp', 'ctx'), may hold values from -6 to 6
- key_in: bfloat16 [8, 512, 1024], P('exp', 'ctx'), may hold values from -6 to 6
- value_in: bfloat16 [8, 512, 2048], P('exp', 'ctx'), may hold values from -6 to 6
- gate_in: bfloat16 [8, 512, 2048], P('exp', 'ctx'), may hold values from -6 to 6
- decay_logit: bfloat16 [8, 512, 16], P('exp', 'ctx'), may hold values from -12 to 0.5
- beta_logit: bfloat16 [8, 512, 16], P('exp', 'ctx'), may hold values from -6 to 6
- head_gain: float32 [128], replicated, may hold values from 0.1 to 1.9
- out_proj: bfloat16 [2048, 2048], P(None, 'ctx'), may hold values from -0.125 to 0.125
Outputs:
- grad_hidden: bfloat16 [8, 512, 2048], P('exp', 'ctx')
- grad_query: bfloat16 [8, 512, 1024], P('exp', 'ctx')
- grad_key: bfloat16 [8, 512, 1024], P('exp', 'ctx')
- grad_value: bfloat16 [8, 512, 2048], P('exp', 'ctx')
- grad_gate: bfloat16 [8, 512, 2048], P('exp', 'ctx')
- grad_decay: bfloat16 [8, 512, 16], P('exp', 'ctx')
- grad_beta: bfloat16 [8, 512, 16], P('exp', 'ctx')
- grad_gate_up: bfloat16 [32, 2048, 1024], P(('ctx', 'exp'))
- grad_down: bfloat16 [32, 512, 2048], P(('ctx', 'exp'))
- grad_out_proj: float32 [2048, 2048], P('exp', 'ctx')
Inputs may be any that keep to these rules, and one draw needn't show every extreme that they name: `route_ids`: each token names 10 different experts. The 128 positions of a sequence on one device name no expert more than 4 times, and one expert below 32, the same on every device, is named exactly 4 times by them.
All inputs are finite; a program needn't handle non-finite values.
Results may differ from a plain program's by a relative error of at most 0.014.
Values may be sent and summed in bfloat16 or wider, within the bound.
A program may use at most 128 MiB of HBM per device.

v0:
```python
import jax
import jax.numpy as jnp
from jax import lax
from jax.sharding import PartitionSpec as P

BLOCK = 128


precise = lax.Precision.HIGHEST


def post_norm(hidden, gains):
    inverse_rms = lax.rsqrt(jnp.mean(hidden * hidden, axis=-1, keepdims=True) + 1e-06)
    return hidden * inverse_rms * gains


def block_step(memory, pieces):
    queries, key_rows, value_rows, strength, log_decay = pieces
    block_len = queries.shape[1]
    positions = jnp.arange(block_len)
    within = positions[:, None] >= positions[None, :]
    strict = positions[:, None] > positions[None, :]
    cumulative = jnp.cumsum(log_decay, axis=1)
    decay_mat = jnp.where(
        within,
        jnp.exp(jnp.where(within, cumulative[:, :, None] - cumulative[:, None, :], 0.0)),
        0.0,
    )
    inner_keys = jnp.einsum("htd,hsd->hts", key_rows, key_rows, precision=precise)
    lower_part = jnp.where(strict, strength[:, :, None] * decay_mat * inner_keys, 0.0)
    system = lower_part + jnp.eye(block_len, dtype=lower_part.dtype)
    recalled = jnp.einsum("hvd,htd->htv", memory, key_rows, precision=precise)
    rising = jnp.exp(cumulative)
    target = strength[:, :, None] * (value_rows - rising[:, :, None] * recalled)
    update = lax.linalg.triangular_solve(
        system, target, left_side=True, lower=True, unit_diagonal=True
    )
    scores = jnp.einsum("htd,hsd->hts", queries, key_rows, precision=precise) * decay_mat
    output = rising[:, :, None] * jnp.einsum("hvd,htd->htv", memory, queries, precision=precise)
    output = output + jnp.einsum("hts,hsv->htv", scores, update, precision=precise)
    last_log = cumulative[:, -1]
    fading = jnp.exp(last_log[:, None] - cumulative)
    memory = jnp.exp(last_log)[:, None, None] * memory + jnp.einsum(
        "hsv,hsd->hvd", update * fading[:, :, None], key_rows, precision=precise
    )
    return (memory, output)


def gated_delta(query_rows, key_rows, value_rows, gate_rows, decay_rows, beta_rows, head_gain):
    length = query_rows.shape[0]
    head_dim = head_gain.shape[0]
    key_heads = query_rows.shape[1] // head_dim
    value_heads = value_rows.shape[1] // head_dim
    group_size = value_heads // key_heads

    def unit_rows(tensor):
        shaped = tensor.reshape(length, key_heads, head_dim)
        shaped = shaped * lax.rsqrt(jnp.sum(shaped * shaped, axis=-1, keepdims=True) + 1e-06)
        return jnp.repeat(shaped, group_size, axis=1)

    queries_unit = unit_rows(query_rows) * head_dim ** (-0.5)
    keys_unit = unit_rows(key_rows)
    values_all = value_rows.reshape(length, value_heads, head_dim)
    strength = jax.nn.sigmoid(beta_rows)
    log_decay = -jax.nn.softplus(decay_rows)
    block_count = length // BLOCK

    def to_blocks(tensor):
        moved_axes = jnp.moveaxis(tensor, 0, 1)
        shaped = moved_axes.reshape((value_heads, block_count, BLOCK) + tensor.shape[2:])
        return jnp.moveaxis(shaped, 1, 0)

    initial = jnp.zeros((value_heads, head_dim, head_dim), query_rows.dtype)
    final_memory, outputs = lax.scan(
        block_step,
        initial,
        (
            to_blocks(queries_unit),
            to_blocks(keys_unit),
            to_blocks(values_all),
            to_blocks(strength),
            to_blocks(log_decay),
        ),
    )
    output = jnp.moveaxis(outputs, 0, 1).reshape(value_heads, length, head_dim)
    output = jnp.moveaxis(output, 0, 1)
    gates_all = gate_rows.reshape(length, value_heads, head_dim)
    normed = (
        output * lax.rsqrt(jnp.mean(output * output, axis=-1, keepdims=True) + 1e-06) * head_gain
    )
    return (normed * jax.nn.silu(gates_all)).reshape(length, value_heads * head_dim)


def expert_backward(rows_in, rows_grad, gate_up, down_proj):
    hidden_units = down_proj.shape[0]
    contract_rows = (((1,), (1,)), ((), ()))
    contract_cols = (((0,), (0,)), ((), ()))
    projected = jnp.dot(rows_in, gate_up, preferred_element_type=jnp.float32)
    gate_part = projected[:, :hidden_units]
    up_part = projected[:, hidden_units:]
    sigma = jax.nn.sigmoid(gate_part)
    activated = gate_part * sigma
    product = (activated * up_part).astype(jnp.bfloat16)
    grad_act = lax.dot_general(
        rows_grad, down_proj, contract_rows, preferred_element_type=jnp.float32
    )
    grad_gate_part = grad_act * up_part * sigma * (1.0 + gate_part * (1.0 - sigma))
    grad_up_part = grad_act * activated
    grad_projected = jnp.concatenate([grad_gate_part, grad_up_part], axis=1).astype(jnp.bfloat16)
    rows_back = lax.dot_general(
        grad_projected, gate_up, contract_rows, preferred_element_type=jnp.float32
    ).astype(jnp.bfloat16)
    weight_gate_up = lax.dot_general(
        rows_in, grad_projected, contract_cols, preferred_element_type=jnp.float32
    ).astype(jnp.bfloat16)
    weight_down = lax.dot_general(
        product, rows_grad, contract_cols, preferred_element_type=jnp.float32
    ).astype(jnp.bfloat16)
    return (rows_back, weight_gate_up, weight_down)


def body(
    hidden_in,
    grad_out,
    post_gain,
    route_ids,
    route_weight,
    gate_up,
    down_proj,
    query_in,
    key_in,
    value_in,
    gate_in,
    decay_logit,
    beta_logit,
    head_gain,
    out_proj,
):
    ctx_count = lax.axis_size("ctx")
    exp_count = lax.axis_size("exp")
    devices = ctx_count * exp_count
    tok_rows = hidden_in.shape[1]
    width = hidden_in.shape[2]
    top_count = route_ids.shape[2]
    capacity = max(3, tok_rows // 32)
    flat_hidden = hidden_in[0].astype(jnp.float32)
    normed, norm_back = jax.vjp(lambda tensor: post_norm(tensor, post_gain), flat_hidden)
    moe_input = normed.astype(jnp.bfloat16)
    slot_ids = route_ids[0].reshape(-1)
    slot_weights = route_weight[0].reshape(-1)
    slot_count = tok_rows * top_count
    owners = jnp.arange(devices, dtype=jnp.int32)
    matches = (slot_ids[:, None] == owners[None, :]).astype(jnp.int32)
    ranks = jnp.sum((jnp.cumsum(matches, axis=0) - 1) * matches, axis=1)
    sentinel = devices * capacity
    destination = jnp.where(slot_ids < devices, slot_ids * capacity + ranks, sentinel)
    source_slot = (
        jnp.full((sentinel,), slot_count, jnp.int32)
        .at[destination]
        .set(jnp.arange(slot_count, dtype=jnp.int32), mode="drop")
    )
    source_token = source_slot // top_count
    input_ext = jnp.concatenate([moe_input, jnp.zeros((1, width), jnp.bfloat16)], axis=0)
    grad_ext = jnp.concatenate([grad_out[0], jnp.zeros((1, width), jnp.bfloat16)], axis=0)
    weight_ext = jnp.concatenate([slot_weights, jnp.zeros((1,), jnp.float32)], axis=0)
    rows_in = input_ext[source_token]
    rows_grad = (
        grad_ext[source_token].astype(jnp.float32) * weight_ext[source_slot][:, None]
    ).astype(jnp.bfloat16)
    flat_shape = (devices, capacity, width)
    got_in, got_grad = (
        lax.all_to_all(
            rows_in.reshape(flat_shape), ("ctx", "exp"), split_axis=0, concat_axis=0, tiled=True
        ),
        lax.all_to_all(
            rows_grad.reshape(flat_shape), ("ctx", "exp"), split_axis=0, concat_axis=0, tiled=True
        ),
    )
    rows_back, grad_gate_up, grad_down = expert_backward(
        got_in.reshape(sentinel, width), got_grad.reshape(sentinel, width), gate_up[0], down_proj[0]
    )
    returned = lax.all_to_all(
        rows_back.reshape(flat_shape), ("ctx", "exp"), split_axis=0, concat_axis=0, tiled=True
    )
    returned_ext = jnp.concatenate(
        [returned.reshape(sentinel, width), jnp.zeros((1, width), jnp.bfloat16)], axis=0
    )
    slot_back = returned_ext[destination].astype(jnp.float32).reshape(tok_rows, top_count, width)
    moe_grad = jnp.sum(slot_back, axis=1)
    (norm_grad,) = norm_back(moe_grad)
    grad_hidden = (grad_out[0].astype(jnp.float32) + norm_grad).astype(jnp.bfloat16)[None]
    query_heads, key_heads, value_heads, gate_heads, decay_heads, beta_heads = (
        lax.all_to_all(query_in, "ctx", split_axis=2, concat_axis=1, tiled=True),
        lax.all_to_all(key_in, "ctx", split_axis=2, concat_axis=1, tiled=True),
        lax.all_to_all(value_in, "ctx", split_axis=2, concat_axis=1, tiled=True),
        lax.all_to_all(gate_in, "ctx", split_axis=2, concat_axis=1, tiled=True),
        lax.all_to_all(decay_logit, "ctx", split_axis=2, concat_axis=1, tiled=True),
        lax.all_to_all(beta_logit, "ctx", split_axis=2, concat_axis=1, tiled=True),
    )

    def forward(query_rows, key_rows, value_rows, gate_rows, decay_rows, beta_rows):
        return gated_delta(
            query_rows, key_rows, value_rows, gate_rows, decay_rows, beta_rows, head_gain
        )

    gated, core_back = jax.vjp(
        forward,
        query_heads[0].astype(jnp.float32),
        key_heads[0].astype(jnp.float32),
        value_heads[0].astype(jnp.float32),
        gate_heads[0].astype(jnp.float32),
        decay_heads[0].astype(jnp.float32),
        beta_heads[0].astype(jnp.float32),
    )
    hidden_all = lax.all_gather(grad_hidden, "ctx", axis=1, tiled=True)[0]
    grad_gated = jnp.dot(hidden_all, out_proj, preferred_element_type=jnp.float32)
    grad_q, grad_k, grad_v, grad_z, grad_d, grad_b = core_back(grad_gated)
    back_query, back_key, back_value, back_gate, back_decay, back_beta = (
        lax.all_to_all(
            grad_q.astype(jnp.bfloat16)[None], "ctx", split_axis=1, concat_axis=2, tiled=True
        ),
        lax.all_to_all(
            grad_k.astype(jnp.bfloat16)[None], "ctx", split_axis=1, concat_axis=2, tiled=True
        ),
        lax.all_to_all(
            grad_v.astype(jnp.bfloat16)[None], "ctx", split_axis=1, concat_axis=2, tiled=True
        ),
        lax.all_to_all(
            grad_z.astype(jnp.bfloat16)[None], "ctx", split_axis=1, concat_axis=2, tiled=True
        ),
        lax.all_to_all(
            grad_d.astype(jnp.bfloat16)[None], "ctx", split_axis=1, concat_axis=2, tiled=True
        ),
        lax.all_to_all(
            grad_b.astype(jnp.bfloat16)[None], "ctx", split_axis=1, concat_axis=2, tiled=True
        ),
    )
    gated_round = gated.astype(jnp.bfloat16)
    scale_factor = float(tok_rows * devices) ** (-0.5)
    grad_out_proj = lax.psum_scatter(
        (
            scale_factor
            * lax.dot_general(
                hidden_all,
                gated_round,
                (((0,), (0,)), ((), ())),
                preferred_element_type=jnp.float32,
            )
        ).astype(jnp.bfloat16),
        "exp",
        scatter_dimension=0,
        tiled=True,
    ).astype(jnp.float32)
    return (
        grad_hidden,
        back_query,
        back_key,
        back_value,
        back_gate,
        back_decay,
        back_beta,
        grad_gate_up[None],
        grad_down[None],
        grad_out_proj,
    )


def solution(mesh):
    placed = (
        P("exp", "ctx", None),
        P("exp", "ctx", None),
        P(),
        P("exp", "ctx", None),
        P("exp", "ctx", None),
        P(("ctx", "exp"), None, None),
        P(("ctx", "exp"), None, None),
        P("exp", "ctx", None),
        P("exp", "ctx", None),
        P("exp", "ctx", None),
        P("exp", "ctx", None),
        P("exp", "ctx", None),
        P("exp", "ctx", None),
        P(),
        P(None, "ctx"),
    )
    return jax.shard_map(
        body,
        mesh=mesh,
        in_specs=placed,
        out_specs=(
            P("exp", "ctx", None),
            P("exp", "ctx", None),
            P("exp", "ctx", None),
            P("exp", "ctx", None),
            P("exp", "ctx", None),
            P("exp", "ctx", None),
            P("exp", "ctx", None),
            P(("ctx", "exp"), None, None),
            P(("ctx", "exp"), None, None),
            P("exp", "ctx"),
        ),
        check_vma=False,
    )
```

profile of v0, /device:TPU:0, one launch (start us, length us, event | category | flops | bytes accessed | tf_op | source)
XLA Modules:
  0.0 807.3 jit_solution(10999468892091857484)
XLA Ops:
  9.8 4.2 all-to-all-start.3
  16.5 9.1 %reduce-window.6 = s32[32,10,128]{2,1,0:T(8,128)S(1)} reduce-window(s32[32,10,128]{2,1,0:T(8,128)S(1)} %fusion.195, s32[]{:T(128)} %constant.224.clone.1), window={size=1x1x128 pad=0_0x0_0x127_0}, to_apply=%region_0.0 | reduce-window | flops 5201920 | bytes 327684 | tf_op jit(solution)/shard_map/reduce-window
  26.9 5.2 scatter_custom_fusion
  61.2 5.1 all-to-all-done.7
  66.3 5.7 all-to-all-start.1
  74.2 12.5 %reduce.13 = bf16[2048,128]{1,0:T(8,128)(2,1)S(1)} reduce(bf16[2048,1,128]{2,1,0:T(2,128)(2,1)} %bitcast.696, bf16[]{:T(256)} %broadcast.678), dimensions={1}, to_apply=%bitcast.472.reduce_sub_computation | reduce | bytes 1048578
  87.6 3.6 copy.619
  91.2 12.5 %reduce.14 = bf16[2048,128]{1,0:T(8,128)(2,1)S(1)} reduce(bf16[2048,1,128]{2,1,0:T(2,128)(2,1)} %bitcast.697, bf16[]{:T(256)} %broadcast.678), dimensions={1}, to_apply=%bitcast.474.reduce_sub_computation | reduce | bytes 1048578
  104.7 4.0 copy.670
  109.2 6.3 all-to-all-start
  124.6 3.9 fusion.163
  140.1 3.7 fusion.166
  144.8 3.6 all-to-all-start.2
  164.8 4.1 all-to-all-start.8
  170.6 6.1 gather_fusion.3
  176.8 10.4 %reshape.875 = f32[128,10,2048]{2,1,0:T(8,128)} reshape(bf16[1280,2048]{1,0:T(8,128)(2,1)} %gather_fusion.3) | data formatting | bytes 15728640 | tf_op jit(solution)/shard_map/convert_element_type | solution.py:188
  187.1 9.8 %reduce_sum.333 = f32[128,2048]{1,0:T(8,128)S(1)} reduce(f32[128,10,2048]{2,1,0:T(8,128)} %reshape.875, f32[]{:T(128)} %constant.232.clone.1), dimensions={1}, to_apply=%region_5.6 | reduce | flops 2359296 | bytes 11534340 | tf_op jit(solution)/shard_map/reduce_sum | solution.py:189
  199.7 224.7 %while.87 = (s32[]{:T(128)}, f32[4,128,128]{2,1,0:T(8,128)S(1)}, f32[4,4,128,128]{3,2,1,0:T(8,128)}, f32[4,4,128,128]{3,2,1,0:T(8,128)}, f32[4,4,128,128]{3,2,1,...) while((s32[]{:T(128)}, f32[4,128,128]{2,1,0:T(8,128)S(1)}, ...), condition=%wide.region_11.12_spmd.clone.clone, body=%wide.region_9.11_spmd.clone.clone.sunk | while | flops 707413120 | bytes 11284438 | solution.py:74
  203.7 39.3 %custom-call.46 = f32[4,1,128,128]{2,3,1,0:T(8,128)S(1)} custom-call(f32[4,1,128,128]{3,2,1,0:T(8,128)S(1)} %add_bitcast_fusion.2), custom_call_target="InvertDiagBlocksLowerTriangular" | custom-call | tf_op jit(solution)/shard_map/jvp()/while/body/eval_jaxpr/triangular_solve | solution.py:35
  259.9 39.3 %custom-call.46 = f32[4,1,128,128]{2,3,1,0:T(8,128)S(1)} custom-call(f32[4,1,128,128]{3,2,1,0:T(8,128)S(1)} %add_bitcast_fusion.2), custom_call_target="InvertDiagBlocksLowerTriangular" | custom-call | tf_op jit(solution)/shard_map/jvp()/while/body/eval_jaxpr/triangular_solve | solution.py:35
  316.1 39.3 %custom-call.46 = f32[4,1,128,128]{2,3,1,0:T(8,128)S(1)} custom-call(f32[4,1,128,128]{3,2,1,0:T(8,128)S(1)} %add_bitcast_fusion.2), custom_call_target="InvertDiagBlocksLowerTriangular" | custom-call | tf_op jit(solution)/shard_map/jvp()/while/body/eval_jaxpr/triangular_solve | solution.py:35
  372.2 39.3 %custom-call.46 = f32[4,1,128,128]{2,3,1,0:T(8,128)S(1)} custom-call(f32[4,1,128,128]{3,2,1,0:T(8,128)S(1)} %add_bitcast_fusion.2), custom_call_target="InvertDiagBlocksLowerTriangular" | custom-call | tf_op jit(solution)/shard_map/jvp()/while/body/eval_jaxpr/triangular_solve | solution.py:35
  433.1 4.1 fusion.187
  446.0 280.8 %while.88 = (s32[]{:T(128)}, f32[4,128,128]{2,1,0:T(8,128)S(1)}, f32[4,4,128,128]{3,2,0,1:T(8,128)}, f32[4,4,128,128]{3,2,0,1:T(8,128)}, bf16[4,4,128,128]{3,2,0...) while((s32[]{:T(128)}, f32[4,128,128]{2,1,0:T(8,128)S(1)}, ...), condition=%wide.region_25.27_spmd.clone.clone, body=%wide.region_14.26_spmd.clone.clone.sunk | while | flops 1513670784 | bytes 36480820 | solution.py:74
  452.2 40.1 %custom-call.47 = f32[4,1,128,128]{2,3,1,0:T(8,128)S(1)} custom-call(f32[4,1,128,128]{3,2,1,0:T(8,128)} %fusion.301), custom_call_target="InvertDiagBlocksLowerTriangular" | custom-call | tf_op jit(solution)/shard_map/transpose(jvp())/while/body/eval_jaxpr/triangular_solve/custom-call.0 | solution.py:35
  522.2 40.1 %custom-call.47 = f32[4,1,128,128]{2,3,1,0:T(8,128)S(1)} custom-call(f32[4,1,128,128]{3,2,1,0:T(8,128)} %fusion.301), custom_call_target="InvertDiagBlocksLowerTriangular" | custom-call | tf_op jit(solution)/shard_map/transpose(jvp())/while/body/eval_jaxpr/triangular_solve/custom-call.0 | solution.py:35
  592.3 40.1 %custom-call.47 = f32[4,1,128,128]{2,3,1,0:T(8,128)S(1)} custom-call(f32[4,1,128,128]{3,2,1,0:T(8,128)} %fusion.301), custom_call_target="InvertDiagBlocksLowerTriangular" | custom-call | tf_op jit(solution)/shard_map/transpose(jvp())/while/body/eval_jaxpr/triangular_solve/custom-call.0 | solution.py:35
  662.3 40.1 %custom-call.47 = f32[4,1,128,128]{2,3,1,0:T(8,128)S(1)} custom-call(f32[4,1,128,128]{3,2,1,0:T(8,128)} %fusion.301), custom_call_target="InvertDiagBlocksLowerTriangular" | custom-call | tf_op jit(solution)/shard_map/transpose(jvp())/while/body/eval_jaxpr/triangular_solve/custom-call.0 | solution.py:35
  756.8 3.6 all-to-all-start.9
  761.5 3.9 reduce.17
  770.9 3.9 reduce.18
  778.8 3.7 all-to-all-start.12
  (578 shorter events, 343.0 us)
Async XLA Ops:
  7.2 130.1 %copy-start = (bf16[1,512,2048]{2,1,0:T(8,128)(2,1)S(1)}, bf16[1,512,2048]{2,1,0:T(8,128)(2,1)}, u32[]{:S(2)}) copy-start(bf16[1,512,2048]{2,1,0:T(8,128)(2,1)} %param.27) | copy-start | bytes 6291460
  7.2 25.0 %copy-start.19 = (bf16[1,128,2048]{2,1,0:T(8,128)(2,1)S(1)}, bf16[1,128,2048]{2,1,0:T(8,128)(2,1)}, u32[]{:S(2)}) copy-start(bf16[1,128,2048]{2,1,0:T(8,128)(2,1)} %param.22) | copy-start | bytes 1572868
  9.8 30.0 %all-to-all-start.3 = ((bf16[4,2,256]{2,1,0:T(2,128)(2,1)}), bf16[4,2,256]{2,1,0:T(2,128)(2,1)S(1)}, u32[]{:S(2)}, u32[]{:S(2)}) async-start(bf16[4,2,256]{2,1,0:T(2,128)(2,1)} %reshape.956), calls=%async_computation.3 | async-start | bytes 8192 | tf_op jit(solution)/shard_map/all_to_all | solution.py:197
  33.2 9.9 %copy-start.38 = (bf16[1,128,1024]{2,1,0:T(8,128)(2,1)S(1)}, bf16[1,128,1024]{2,1,0:T(8,128)(2,1)}, u32[]{:S(2)}) copy-start(bf16[1,128,1024]{2,1,0:T(8,128)(2,1)} %param.29) | copy-start | bytes 786436
  36.0 14.3 %copy-start.39 = (f32[2048]{0:T(1024)S(1)}, f32[2048]{0:T(1024)}, u32[]{:S(2)}) copy-start(f32[2048]{0:T(1024)} %param.23) | copy-start | bytes 24580
  39.8 7.1 all-to-all-start.4
  46.9 9.8 %all-to-all-start.5 = ((bf16[4,2,16384]{2,1,0:T(2,128)(2,1)}), bf16[4,2,16384]{2,1,0:T(2,128)(2,1)S(1)}, u32[]{:S(2)}, u32[]{:S(2)}) async-start(bf16[4,2,16384]{2,1,0:T(2,128)(2,1)} %reshape.960), calls=%async_computation.5 | async-start | bytes 524288 | tf_op jit(solution)/shard_map/all_to_all | solution.py:194
  56.7 15.5 %copy-start.33 = (bf16[1,128,2048]{2,1,0:T(8,128)(2,1)S(1)}, bf16[1,128,2048]{2,1,0:T(8,128)(2,1)}, u32[]{:S(2)}) copy-start(bf16[1,128,2048]{2,1,0:T(8,128)(2,1)} %param.30) | copy-start | bytes 1572868
  56.7 30.0 %copy-start.28 = (bf16[4,2,16384]{2,1,0:T(2,128)(2,1)}, bf16[4,2,16384]{2,1,0:T(2,128)(2,1)S(1)}, u32[]{:S(2)}) copy-start(bf16[4,2,16384]{2,1,0:T(2,128)(2,1)S(1)} %all-to-all-done.5) | copy-start | bytes 786436
  56.7 9.5 %all-to-all-start.7 = ((bf16[4,2,16384]{2,1,0:T(2,128)(2,1)}), bf16[4,2,16384]{2,1,0:T(2,128)(2,1)S(1)}, u32[]{:S(2)}, u32[]{:S(2)}) async-start(bf16[4,2,16384]{2,1,0:T(2,128)(2,1)} %reshape.954), calls=%async_computation.7 | async-start | bytes 524288 | tf_op jit(solution)/shard_map/all_to_all | solution.py:193
  66.3 43.0 %all-to-all-start.1 = ((bf16[32,4,2048]{2,1,0:T(4,128)(2,1)}), bf16[32,4,2048]{2,1,0:T(4,128)(2,1)}, u32[]{:S(2)}, u32[]{:S(2)}) async-start(bf16[32,4,2048]{2,1,0:T(4,128)(2,1)} %reshape.853), calls=%async_computation.1 | async-start | bytes 1048576 | tf_op jit(solution)/shard_map/all_to_all | solution.py:172
  109.2 22.7 %all-to-all-start = ((bf16[32,4,2048]{2,1,0:T(4,128)(2,1)}), bf16[32,4,2048]{2,1,0:T(4,128)(2,1)}, u32[]{:S(2)}, u32[]{:S(2)}) async-start(bf16[32,4,2048]{2,1,0:T(4,128)(2,1)} %multiply_convert_fusion.2), calls=%async_computation | async-start | bytes 1048576 | tf_op jit(solution)/shard_map/all_to_all | solution.py:175
  131.9 12.9 %all-to-all-start.6 = ((bf16[4,2,32768]{2,1,0:T(2,128)(2,1)}), bf16[4,2,32768]{2,1,0:T(2,128)(2,1)S(1)}, u32[]{:S(2)}, u32[]{:S(2)}) async-start(bf16[4,2,32768]{2,1,0:T(2,128)(2,1)} %reshape.962), calls=%async_computation.6 | async-start | bytes 1048576 | tf_op jit(solution)/shard_map/all_to_all | solution.py:195
  144.8 20.0 %all-to-all-start.2 = ((bf16[32,4,2048]{2,1,0:T(4,128)(2,1)}), bf16[32,4,2048]{2,1,0:T(4,128)(2,1)}, u32[]{:S(2)}, u32[]{:S(2)}) async-start(bf16[32,4,2048]{2,1,0:T(4,128)(2,1)} %reshape.855), calls=%async_computation.2 | async-start | bytes 1048576 | tf_op jit(solution)/shard_map/all_to_all | solution.py:182
  164.8 262.7 %all-to-all-start.8 = ((bf16[4,2,32768]{2,1,0:T(2,128)(2,1)}), bf16[4,2,32768]{2,1,0:T(2,128)(2,1)}, u32[]{:S(2)}, u32[]{:S(2)}) async-start(bf16[4,2,32768]{2,1,0:T(2,128)(2,1)} %reshape.964), calls=%async_computation.8 | async-start | bytes 1048576 | tf_op jit(solution)/shard_map/all_to_all | solution.py:196
  168.9 264.2 %all-gather.2.cloned.1.call-start = ((), (), s32[]{:S(2)}) async-start(), calls=%async_computation.16 | async-start | bytes 2621440 | tf_op jit(solution)/shard_map/all_gather | solution.py:215
  187.1 9.8 %copy-start.9 = (bf16[1,128,2048]{2,1,0:T(8,128)(2,1)S(1)}, bf16[1,128,2048]{2,1,0:T(8,128)(2,1)}, u32[]{:S(2)}) copy-start(bf16[1,128,2048]{2,1,0:T(8,128)(2,1)} %param.21) | copy-start | bytes 1572868
  199.5 599.0 %reduce-scatter.2.cloned.1.call-start = ((), (), s32[]{:S(2)}) async-start(), calls=%async_computation.17 | async-start | bytes 2359296 | tf_op jit(solution)/shard_map/reduce_scatter | solution.py:240
  726.9 7.9 copy-start.13
  729.4 10.7 %all-to-all-start.13 = ((bf16[4,2,256]{2,1,0:T(2,128)(2,1)}), bf16[4,2,256]{2,1,0:T(2,128)(2,1)S(1)}, u32[]{:S(2)}, u32[]{:S(2)}) async-start(bf16[4,2,256]{2,1,0:T(2,128)(2,1)} %reshape.974), calls=%async_computation.13 | async-start | bytes 8192 | tf_op jit(solution)/shard_map/all_to_all | solution.py:231
  740.1 7.2 all-to-all-start.14
  747.3 9.4 %all-to-all-start.10 = ((bf16[4,2,16384]{2,1,0:T(2,128)(2,1)}), bf16[4,2,16384]{2,1,0:T(2,128)(2,1)S(1)}, u32[]{:S(2)}, u32[]{:S(2)}) async-start(bf16[4,2,16384]{2,1,0:T(2,128)(2,1)} %reshape.968), calls=%async_computation.10 | async-start | bytes 524288 | tf_op jit(solution)/shard_map/all_to_all | solution.py:222
  750.8 9.6 %copy-start.24 = (bf16[4,4,128,128]{3,2,0,1:T(8,128)(2,1)S(1)}, bf16[4,4,128,128]{3,2,0,1:T(8,128)(2,1)}, u32[]{:S(2)}) copy-start(bf16[4,4,128,128]{3,2,0,1:T(8,128)(2,1)} %get-tuple-element.1274) | copy-start | bytes 1572868
  756.8 9.8 %all-to-all-start.9 = ((bf16[4,2,16384]{2,1,0:T(2,128)(2,1)}), bf16[4,2,16384]{2,1,0:T(2,128)(2,1)S(1)}, u32[]{:S(2)}, u32[]{:S(2)}) async-start(bf16[4,2,16384]{2,1,0:T(2,128)(2,1)} %reshape.966), calls=%async_computation.9 | async-start | bytes 524288 | tf_op jit(solution)/shard_map/all_to_all | solution.py:219
  761.5 8.5 %copy-start.26 = (bf16[512,4,128]{0,2,1:T(8,128)(2,1)S(1)}, bf16[512,4,128]{0,2,1:T(8,128)(2,1)}, u32[]{:S(2)}) copy-start(bf16[512,4,128]{0,2,1:T(8,128)(2,1)} %get-tuple-element.2412) | copy-start | bytes 1572868
  766.5 12.3 %all-to-all-start.11 = ((bf16[4,2,32768]{2,1,0:T(2,128)(2,1)}), bf16[4,2,32768]{2,1,0:T(2,128)(2,1)S(1)}, u32[]{:S(2)}, u32[]{:S(2)}) async-start(bf16[4,2,32768]{2,1,0:T(2,128)(2,1)} %reshape.970), calls=%async_computation.11 | async-start | bytes 1048576 | tf_op jit(solution)/shard_map/all_to_all | solution.py:225
  770.9 11.6 %copy-start.25 = (bf16[128,2048]{1,0:T(8,128)(2,1)S(1)}, bf16[128,2048]{1,0:T(8,128)(2,1)}, u32[]{:S(2)}) copy-start(bf16[128,2048]{1,0:T(8,128)(2,1)} %reshape.852) | copy-start | bytes 1572868
  770.9 11.6 %copy-start.27 = (f32[128,1024]{1,0:T(8,128)S(1)}, f32[128,1024]{1,0:T(8,128)}, u32[]{:S(2)}) copy-start(f32[128,1024]{1,0:T(8,128)} %fusion.163) | copy-start | bytes 1572868
  776.0 8.6 %copy-start.10 = (bf16[128,2048]{1,0:T(8,128)(2,1)S(1)}, bf16[128,2048]{1,0:T(8,128)(2,1)}, u32[]{:S(2)}) copy-start(bf16[128,2048]{1,0:T(8,128)(2,1)} %reshape.854) | copy-start | bytes 1572868
  776.0 8.6 %copy-start.35 = (bf16[128,512]{1,0:T(8,128)(2,1)S(1)}, bf16[128,512]{1,0:T(8,128)(2,1)}, u32[]{:S(2)}) copy-start(bf16[128,512]{1,0:T(8,128)(2,1)} %copy-done.34) | copy-start | bytes 393220
  776.0 8.6 %copy-start.37 = (bf16[128,512]{1,0:T(8,128)(2,1)S(1)}, bf16[128,512]{1,0:T(8,128)(2,1)}, u32[]{:S(2)}) copy-start(bf16[128,512]{1,0:T(8,128)(2,1)} %copy-done.36) | copy-start | bytes 393220
  778.8 15.9 %all-to-all-start.12 = ((bf16[4,2,32768]{2,1,0:T(2,128)(2,1)}), bf16[4,2,32768]{2,1,0:T(2,128)(2,1)S(1)}, u32[]{:S(2)}, u32[]{:S(2)}) async-start(bf16[4,2,32768]{2,1,0:T(2,128)(2,1)} %reshape.972), calls=%async_computation.12 | async-start | bytes 1048576 | tf_op jit(solution)/shard_map/all_to_all | solution.py:228
  (44 other events, 150.6 us)
Sparse Core Ops, SparseCore 0:
  199.6 24.0 all-gather.1
  442.1 69.5 reduce-scatter.1
where the time goes:
time: 819 us; the launch traced here: 807 us
  other arithmetic  433 us (53%)
  matrix products  147 us (18%)
  local copies, waits for them, and re-layouts  136 us (17%)
  starting transfers between devices  59.1 us (7%)
  between operations  15.7 us (2%)
  waiting for transfers between devices  14.4 us (2%)
    another operation x32, other arithmetic, block_step(): lax.linalg.triangular_solve(system, target, left_side=True, lower=True, u...  326 us
    unnamed x15, other arithmetic  46.7 us
    unnamed x121, local copies, waits for them, and re-layouts  37.3 us
    dot_general x12, matrix products, block_step(): jnp.einsum('htd,hsd->hts', queries, key_rows, precision=precise) * decay_mat  25.9 us
    another operation x12, matrix products, block_step(): lax.linalg.triangular_solve(system, target, left_side=True, lower=True, u...  25.9 us
    dot_general x12, matrix products, block_step(): jnp.einsum('hts,hsv->htv', scores, update, precision=precise)  18.7 us
    dot_general x12, matrix products, block_step(): jnp.einsum('hvd,htd->htv', memory, queries, precision=precise)  17.6 us
  transfers between devices with their start and end apart: 17, of which 6 were waited for; matrix products, arithmetic and copies ran while one was open for 87% of the time, Pallas kernels for 0%

commit v1 on v0

v1 whole, which is shorter than its diff:
```python
import functools

import jax
import jax.numpy as jnp
from jax import lax
from jax.experimental import pallas as pl
from jax.experimental.pallas import tpu as pltpu
from jax.sharding import PartitionSpec as P

BLOCK = 128
LANES = 128
f32 = jnp.float32
bf16 = jnp.bfloat16


def split(tensor):
    high = tensor.astype(bf16)
    return high, (tensor - high.astype(f32)).astype(bf16)


def full(left, right):
    return [(left[0], right[0]), (left[1], right[0]), (left[0], right[1])]


def left_exact(left, right):
    return [(left, right[0]), (left, right[1])]


def right_exact(left, right):
    return [(left[0], right), (left[1], right)]


def contract(pairs, left_dim, right_dim):
    left = jnp.concatenate([pair[0] for pair in pairs], axis=left_dim)
    right = jnp.concatenate([pair[1] for pair in pairs], axis=right_dim)
    return lax.dot_general(
        left, right, (((left_dim,), (right_dim,)), ((), ())), preferred_element_type=f32
    )


def sigmoid(tensor):
    return 1.0 / (1.0 + jnp.exp(-tensor))


def row_sum(tensor):
    return jnp.sum(tensor, axis=1, keepdims=True)


def offsets(key_heads, value_heads):
    query_at = 0
    key_at = key_heads * LANES
    value_at = 2 * key_heads * LANES
    gate_at = value_at + value_heads * LANES
    small_at = gate_at + value_heads * LANES
    return query_at, key_at, value_at, gate_at, small_at


def shared(x_ref, key_heads, value_heads):
    query_at, key_at, _, _, small_at = offsets(key_heads, value_heads)
    row = lax.broadcasted_iota(jnp.int32, (BLOCK, BLOCK), 0)
    col = lax.broadcasted_iota(jnp.int32, (BLOCK, BLOCK), 1)
    within = row >= col
    small = x_ref[:, small_at : small_at + LANES].astype(f32)
    log_decay = -(jnp.maximum(small, 0.0) + jnp.log1p(jnp.exp(-jnp.abs(small))))
    log_decay = jnp.where(col < value_heads, log_decay, 0.0)
    cumulative = jnp.dot(
        within.astype(f32),
        log_decay,
        precision=lax.Precision.HIGHEST,
        preferred_element_type=f32,
    )
    strengths = sigmoid(small)
    keys, queries = [], []
    packed = cumulative
    for j in range(key_heads):
        q = x_ref[:, query_at + j * LANES : query_at + (j + 1) * LANES]
        k = x_ref[:, key_at + j * LANES : key_at + (j + 1) * LANES]
        qf, kf = q.astype(f32), k.astype(f32)
        q_norm = lax.rsqrt(row_sum(qf * qf) + 1e-06)
        k_norm = lax.rsqrt(row_sum(kf * kf) + 1e-06)
        queries.append((q, q_norm))
        keys.append((k, k_norm))
        packed = jnp.where(col == 2 * value_heads + j, k_norm, packed)
    turned = packed.T
    grams = []
    for j in range(key_heads):
        (q, q_norm), (k, k_norm) = queries[j], keys[j]
        k_row = turned[2 * value_heads + j : 2 * value_heads + j + 1, :]
        kk = contract([(k, k)], 1, 1) * k_norm * k_row
        qk = contract([(q, k)], 1, 1) * (q_norm * LANES ** (-0.5)) * k_row
        grams.append((kk, qk, k_row))
    heads = []
    for i in range(value_heads):
        g = cumulative[:, i : i + 1]
        last = cumulative[BLOCK - 1 : BLOCK, i : i + 1]
        decay = jnp.where(within, jnp.exp(jnp.minimum(g - turned[i : i + 1, :], 0.0)), 0.0)
        beta = strengths[:, value_heads + i : value_heads + i + 1]
        heads.append((decay, beta, jnp.exp(g), jnp.exp(last - g), jnp.exp(last)))
    return row, col, small, strengths, queries, keys, grams, heads


def forward_kernel(
    key_heads, value_heads, x_ref, gain_ref, t_ref, u_ref, h_ref, o_ref, gated_ref, state
):
    group = value_heads // key_heads
    _, _, value_at, gate_at, _ = offsets(key_heads, value_heads)

    @pl.when(pl.program_id(0) == 0)
    def _():
        state[...] = jnp.zeros_like(state)

    row, col, _, _, queries, keys, grams, heads = shared(x_ref, key_heads, value_heads)
    every = range(value_heads)
    strict = row > col
    lower = [
        jnp.where(strict, heads[i][1] * heads[i][0] * grams[i // group][0], 0.0) for i in every
    ]
    eye = (row == col).astype(f32)
    mask = (row >> 1) == (col >> 1)
    inverse = [eye - jnp.where(mask, lower[i], 0.0) for i in every]
    level = 1
    while (1 << level) < BLOCK:
        mask = ((row >> (level + 1)) == (col >> (level + 1))) & ((row >> level) != (col >> level))
        halves = [split(inverse[i]) for i in every]
        middle = [
            contract(full(split(jnp.where(mask, lower[i], 0.0)), halves[i]), 1, 0) for i in every
        ]
        inverse = [
            inverse[i] - contract(full(halves[i], split(middle[i])), 1, 0) for i in every
        ]
        level += 1
    memory = [state[i] for i in every]
    memory_halves = [split(memory[i]) for i in every]
    recalled = [
        contract(left_exact(keys[i // group][0], memory_halves[i]), 1, 0) * keys[i // group][1]
        for i in every
    ]
    asked = [
        contract(left_exact(queries[i // group][0], memory_halves[i]), 1, 0)
        * (queries[i // group][1] * LANES ** (-0.5))
        for i in every
    ]
    target = []
    for i in every:
        _, beta, rising, _, _ = heads[i]
        values = x_ref[:, value_at + i * LANES : value_at + (i + 1) * LANES].astype(f32)
        target.append(beta * (values - rising * recalled[i]))
    update = [contract(full(split(inverse[i]), split(target[i])), 1, 0) for i in every]
    output = [
        heads[i][2] * asked[i]
        + contract(full(split(grams[i // group][1] * heads[i][0]), split(update[i])), 1, 0)
        for i in every
    ]
    for i in every:
        _, _, _, fading, whole = heads[i]
        key, key_norm = keys[i // group]
        t_ref[0, i] = inverse[i]
        u_ref[0, i] = update[i]
        h_ref[0, i] = memory[i]
        o_ref[0, i] = output[i]
        state[i] = whole * memory[i] + contract(
            left_exact(key, split(key_norm * fading * update[i])), 0, 0
        )
        gate = x_ref[:, gate_at + i * LANES : gate_at + (i + 1) * LANES].astype(f32)
        scale = lax.rsqrt(row_sum(output[i] * output[i]) * (1.0 / LANES) + 1e-06)
        gated = output[i] * scale * gain_ref[...] * (gate * sigmoid(gate))
        gated_ref[:, i * LANES : (i + 1) * LANES] = gated.astype(bf16)


def backward_kernel(
    key_heads, value_heads, x_ref, gain_ref, t_ref, u_ref, h_ref, o_ref, grad_ref, y_ref, state
):
    group = value_heads // key_heads
    query_at, key_at, value_at, gate_at, small_at = offsets(key_heads, value_heads)

    @pl.when(pl.program_id(0) == 0)
    def _():
        state[...] = jnp.zeros_like(state)

    row, col, small, strengths, queries, keys, grams, heads = shared(
        x_ref, key_heads, value_heads
    )
    every = range(value_heads)
    strict = row > col
    scale_q = LANES ** (-0.5)
    grad_o = []
    for i in every:
        gate = x_ref[:, gate_at + i * LANES : gate_at + (i + 1) * LANES].astype(f32)
        sigma = sigmoid(gate)
        output = o_ref[0, i]
        inverse_rms = lax.rsqrt(row_sum(output * output) * (1.0 / LANES) + 1e-06)
        normed = output * inverse_rms
        grad = grad_ref[:, i * LANES : (i + 1) * LANES]
        grad_z = grad * normed * gain_ref[...] * (sigma * (1.0 + gate * (1.0 - sigma)))
        y_ref[:, gate_at + i * LANES : gate_at + (i + 1) * LANES] = grad_z.astype(bf16)
        grad_n = grad * gain_ref[...] * (gate * sigma)
        grad_o.append(
            inverse_rms * (grad_n - normed * (row_sum(grad_n * normed) * (1.0 / LANES)))
        )
    grad_h = [state[i] for i in every]
    grad_h2 = [split(grad_h[i]) for i in every]
    grad_o2 = [split(grad_o[i]) for i in every]
    memory = [h_ref[0, i] for i in every]
    memory2 = [split(memory[i]) for i in every]
    update = [u_ref[0, i] for i in every]
    update2 = [split(update[i]) for i in every]
    scores = [grams[i // group][1] * heads[i][0] for i in every]
    key_grad_h = [
        contract(left_exact(keys[i // group][0], grad_h2[i]), 1, 0) * keys[i // group][1]
        for i in every
    ]
    grad_u = [
        contract(full(split(scores[i]), grad_o2[i]), 0, 0) + heads[i][3] * key_grad_h[i]
        for i in every
    ]
    grad_t = [contract(full(split(t_ref[0, i]), split(grad_u[i])), 0, 0) for i in every]
    grad_p = [contract(full(grad_o2[i], update2[i]), 1, 1) for i in every]
    grad_a = [
        jnp.where(strict, -contract(full(split(grad_t[i]), update2[i]), 1, 1), 0.0) for i in every
    ]
    recalled = [
        contract(left_exact(keys[i // group][0], memory2[i]), 1, 0) * keys[i // group][1]
        for i in every
    ]
    asked = [
        contract(left_exact(queries[i // group][0], memory2[i]), 1, 0)
        * (queries[i // group][1] * scale_q)
        for i in every
    ]
    grad_q = [None] * key_heads
    grad_k = [None] * key_heads
    grad_beta = jnp.zeros((BLOCK, LANES), f32)
    grad_g = jnp.zeros((BLOCK, LANES), f32)
    column_sums = jnp.zeros((BLOCK, LANES), f32)

    def add(total, term):
        return term if total is None else total + term

    for i in every:
        j = i // group
        decay, beta, rising, fading, whole = heads[i]
        (q, q_norm), (k, k_norm) = queries[j], keys[j]
        q_scale = q_norm * scale_q
        kk, _, k_row = grams[j]
        values = x_ref[:, value_at + i * LANES : value_at + (i + 1) * LANES].astype(f32)
        grad_w = beta * grad_t[i]
        y_ref[:, value_at + i * LANES : value_at + (i + 1) * LANES] = grad_w.astype(bf16)
        decayed = decay * kk
        beta_term = row_sum(grad_t[i] * (values - rising * recalled[i])) + row_sum(
            grad_a[i] * decayed
        )
        grad_beta = jnp.where(col == value_heads + i, beta_term, grad_beta)
        pulled = grad_p[i] * scores[i] + grad_a[i] * (beta * decayed)
        fade_term = fading * row_sum(update[i] * key_grad_h[i])
        rise_term = rising * (row_sum(grad_o[i] * asked[i]) - row_sum(grad_w * recalled[i]))
        last_term = jnp.sum(fade_term, axis=0, keepdims=True) + whole * jnp.sum(
            row_sum(memory[i] * grad_h[i]), axis=0, keepdims=True
        )
        g_term = row_sum(pulled) + rise_term - fade_term
        g_term = g_term + jnp.where(row[:, :1] == BLOCK - 1, last_term, 0.0)
        grad_g = jnp.where(col == i, g_term, grad_g)
        column_sums = jnp.where(row == i, jnp.sum(pulled, axis=0, keepdims=True), column_sums)
        grad_qk = grad_p[i] * decay
        grad_kk = grad_a[i] * (beta * decay)
        grad_kh = -rising * grad_w
        risen = rising * grad_o[i]
        grad_q[j] = add(
            grad_q[j],
            contract(
                full(split(risen), memory2[i]), 1, 1
            )
            + contract(right_exact(split(grad_qk * k_row), k), 1, 0),
        )
        grad_k[j] = add(
            grad_k[j],
            contract(
                full(split(grad_kh), memory2[i]) + full(split(fading * update[i]), grad_h2[i]), 1, 1
            )
            + contract(right_exact(split(grad_kk * k_row), k), 1, 0)
            + contract(
                right_exact(split(grad_qk * q_scale), q) + right_exact(split(grad_kk * k_norm), k),
                0,
                0,
            ),
        )
        state[i] = whole * grad_h[i] + contract(
            left_exact(k, split(k_norm * grad_kh)) + left_exact(q, split(q_scale * risen)), 0, 0
        )
    for j in range(key_heads):
        (q, q_norm), (k, k_norm) = queries[j], keys[j]
        unit = q.astype(f32) * q_norm
        grad = grad_q[j] * scale_q
        grad = q_norm * (grad - unit * row_sum(unit * grad))
        y_ref[:, query_at + j * LANES : query_at + (j + 1) * LANES] = grad.astype(bf16)
        unit = k.astype(f32) * k_norm
        grad = k_norm * (grad_k[j] - unit * row_sum(unit * grad_k[j]))
        y_ref[:, key_at + j * LANES : key_at + (j + 1) * LANES] = grad.astype(bf16)
    grad_g = grad_g - column_sums.T
    grad_log = jnp.dot(
        (row <= col).astype(f32),
        grad_g,
        precision=lax.Precision.HIGHEST,
        preferred_element_type=f32,
    )
    small_grad = jnp.where(
        col < value_heads, -grad_log * strengths, grad_beta * strengths * (1.0 - strengths)
    )
    y_ref[:, small_at : small_at + LANES] = small_grad.astype(bf16)


def residual_spec(value_heads, place):
    return pl.BlockSpec((1, value_heads, BLOCK, LANES), lambda c: (place(c), 0, 0, 0))


def delta_forward(x, gain, key_heads, value_heads):
    length, columns = x.shape
    blocks = length // BLOCK
    kept = jax.ShapeDtypeStruct((blocks, value_heads, BLOCK, LANES), f32)
    passes = blocks * value_heads * 36
    return pl.pallas_call(
        functools.partial(forward_kernel, key_heads, value_heads),
        grid=(blocks,),
        out_shape=(kept,) * 4 + (jax.ShapeDtypeStruct((length, value_heads * LANES), bf16),),
        in_specs=[
            pl.BlockSpec((BLOCK, columns), lambda c: (c, 0)),
            pl.BlockSpec((1, LANES), lambda c: (0, 0)),
        ],
        out_specs=[residual_spec(value_heads, lambda c: c)] * 4
        + [pl.BlockSpec((BLOCK, value_heads * LANES), lambda c: (c, 0))],
        scratch_shapes=[pltpu.VMEM((value_heads, LANES, LANES), f32)],
        compiler_params=pltpu.CompilerParams(vmem_limit_bytes=40 * 2**20),
        cost_estimate=pl.CostEstimate(
            flops=passes * 8 * LANES**3, bytes_accessed=6 * 2**20, transcendentals=2**20
        ),
    )(x, gain)


def delta_backward(x, gain, kept, grad_gated, key_heads, value_heads):
    length, columns = x.shape
    blocks = length // BLOCK

    def place(c):
        return blocks - 1 - c

    passes = blocks * value_heads * 30
    return pl.pallas_call(
        functools.partial(backward_kernel, key_heads, value_heads),
        grid=(blocks,),
        out_shape=jax.ShapeDtypeStruct((length, columns), bf16),
        in_specs=[
            pl.BlockSpec((BLOCK, columns), lambda c: (place(c), 0)),
            pl.BlockSpec((1, LANES), lambda c: (0, 0)),
        ]
        + [residual_spec(value_heads, place)] * 4
        + [pl.BlockSpec((BLOCK, value_heads * LANES), lambda c: (place(c), 0))],
        out_specs=pl.BlockSpec((BLOCK, columns), lambda c: (place(c), 0)),
        scratch_shapes=[pltpu.VMEM((value_heads, LANES, LANES), f32)],
        compiler_params=pltpu.CompilerParams(vmem_limit_bytes=40 * 2**20),
        cost_estimate=pl.CostEstimate(
            flops=passes * 8 * LANES**3, bytes_accessed=8 * 2**20, transcendentals=2**20
        ),
    )(x, gain, *kept, grad_gated)


def post_norm(hidden, gains):
    inverse_rms = lax.rsqrt(jnp.mean(hidden * hidden, axis=-1, keepdims=True) + 1e-06)
    return hidden * inverse_rms * gains


def expert_backward(rows_in, rows_grad, gate_up, down_proj):
    hidden_units = down_proj.shape[0]
    contract_rows = (((1,), (1,)), ((), ()))
    contract_cols = (((0,), (0,)), ((), ()))
    projected = jnp.dot(rows_in, gate_up, preferred_element_type=jnp.float32)
    gate_part = projected[:, :hidden_units]
    up_part = projected[:, hidden_units:]
    sigma = jax.nn.sigmoid(gate_part)
    activated = gate_part * sigma
    product = (activated * up_part).astype(jnp.bfloat16)
    grad_act = lax.dot_general(
        rows_grad, down_proj, contract_rows, preferred_element_type=jnp.float32
    )
    grad_gate_part = grad_act * up_part * sigma * (1.0 + gate_part * (1.0 - sigma))
    grad_up_part = grad_act * activated
    grad_projected = jnp.concatenate([grad_gate_part, grad_up_part], axis=1).astype(jnp.bfloat16)
    rows_back = lax.dot_general(
        grad_projected, gate_up, contract_rows, preferred_element_type=jnp.float32
    ).astype(jnp.bfloat16)
    weight_gate_up = lax.dot_general(
        rows_in, grad_projected, contract_cols, preferred_element_type=jnp.float32
    ).astype(jnp.bfloat16)
    weight_down = lax.dot_general(
        product, rows_grad, contract_cols, preferred_element_type=jnp.float32
    ).astype(jnp.bfloat16)
    return (rows_back, weight_gate_up, weight_down)

def body(
    hidden_in,
    grad_out,
    post_gain,
    route_ids,
    route_weight,
    gate_up,
    down_proj,
    query_in,
    key_in,
    value_in,
    gate_in,
    decay_logit,
    beta_logit,
    head_gain,
    out_proj,
):
    ctx_count = lax.axis_size("ctx")
    exp_count = lax.axis_size("exp")
    devices = ctx_count * exp_count
    tok_rows = hidden_in.shape[1]
    width = hidden_in.shape[2]
    capacity = max(3, tok_rows // 32)
    key_heads = query_in.shape[2] // LANES // ctx_count
    value_heads = value_in.shape[2] // LANES // ctx_count
    slots = devices * capacity

    def by_device(tensor):
        return tensor[0].reshape(tok_rows, ctx_count, -1)

    packed = [by_device(t) for t in (query_in, key_in, value_in, gate_in, decay_logit, beta_logit)]
    packed.append(jnp.zeros((tok_rows, ctx_count, LANES - 2 * value_heads), bf16))
    outgoing = jnp.concatenate(packed, axis=2).transpose(1, 0, 2)
    columns = outgoing.shape[2]

    flat_hidden = hidden_in[0].astype(f32)
    normed, norm_back = jax.vjp(lambda tensor: post_norm(tensor, post_gain), flat_hidden)
    moe_input = normed.astype(bf16)
    owners = jnp.arange(devices, dtype=jnp.int32)
    named = route_ids[0][:, :, None] == owners[None, None, :]
    picked = jnp.any(named, axis=1)
    weights = jnp.sum(jnp.where(named, route_weight[0][:, :, None], 0.0), axis=1)
    positions = jnp.arange(tok_rows)
    earlier = (positions[:, None] > positions[None, :]).astype(bf16)
    ranks = jnp.dot(earlier, picked.astype(bf16), preferred_element_type=f32)
    places = jnp.arange(capacity, dtype=f32)
    chosen = picked.T[:, None, :] & (ranks.T[:, None, :] == places[None, :, None])
    slot_weight = jnp.sum(jnp.where(chosen, weights.T[:, None, :], 0.0), axis=2).reshape(slots, 1)
    chosen = chosen.reshape(slots, tok_rows).astype(bf16)
    rows_in = jnp.dot(chosen, moe_input, preferred_element_type=f32).astype(bf16)
    rows_grad = (
        jnp.dot(chosen, grad_out[0], preferred_element_type=f32) * slot_weight
    ).astype(bf16)
    sent = jnp.concatenate([rows_in, rows_grad], axis=1).reshape(devices, capacity, 2 * width)
    got = lax.all_to_all(sent, ("ctx", "exp"), split_axis=0, concat_axis=0, tiled=True)
    got = got.reshape(slots, 2 * width)
    x = lax.all_to_all(outgoing, "ctx", split_axis=0, concat_axis=0, tiled=True)
    x = x.reshape(ctx_count * tok_rows, columns)
    gain = head_gain[None, :]
    *kept, gated_round = delta_forward(x, gain, key_heads, value_heads)
    rows_back, grad_gate_up, grad_down = expert_backward(
        got[:, :width], got[:, width:], gate_up[0], down_proj[0]
    )
    returned = lax.all_to_all(
        rows_back.reshape(devices, capacity, width),
        ("ctx", "exp"),
        split_axis=0,
        concat_axis=0,
        tiled=True,
    ).reshape(slots, width)
    moe_grad = lax.dot_general(
        chosen, returned, (((0,), (0,)), ((), ())), preferred_element_type=f32
    )
    (norm_grad,) = norm_back(moe_grad)
    grad_hidden = (grad_out[0].astype(f32) + norm_grad).astype(bf16)[None]
    hidden_all = lax.all_gather(grad_hidden, "ctx", axis=1, tiled=True)[0]
    grad_gated = jnp.dot(hidden_all, out_proj, preferred_element_type=f32)
    y = delta_backward(x, gain, kept, grad_gated, key_heads, value_heads)
    scale_factor = float(tok_rows * devices) ** (-0.5)
    grad_out_proj = lax.psum_scatter(
        (
            scale_factor
            * lax.dot_general(
                hidden_all, gated_round, (((0,), (0,)), ((), ())), preferred_element_type=f32
            )
        ).astype(bf16),
        "exp",
        scatter_dimension=0,
        tiled=True,
    ).astype(f32)
    back = lax.all_to_all(
        y.reshape(ctx_count, tok_rows, columns), "ctx", split_axis=0, concat_axis=0, tiled=True
    )
    parts, start = [], 0
    for count in [key_heads * LANES] * 2 + [value_heads * LANES] * 2 + [value_heads] * 2:
        part = back[:, :, start : start + count].transpose(1, 0, 2)
        parts.append(part.reshape(1, tok_rows, ctx_count * count))
        start += count
    return (grad_hidden, *parts, grad_gate_up[None], grad_down[None], grad_out_proj)


def solution(mesh):
    placed = (
        P("exp", "ctx", None),
        P("exp", "ctx", None),
        P(),
        P("exp", "ctx", None),
        P("exp", "ctx", None),
        P(("ctx", "exp"), None, None),
        P(("ctx", "exp"), None, None),
        P("exp", "ctx", None),
        P("exp", "ctx", None),
        P("exp", "ctx", None),
        P("exp", "ctx", None),
        P("exp", "ctx", None),
        P("exp", "ctx", None),
        P(),
        P(None, "ctx"),
    )
    return jax.shard_map(
        body,
        mesh=mesh,
        in_specs=placed,
        out_specs=(
            P("exp", "ctx", None),
            P("exp", "ctx", None),
            P("exp", "ctx", None),
            P("exp", "ctx", None),
            P("exp", "ctx", None),
            P("exp", "ctx", None),
            P("exp", "ctx", None),
            P(("ctx", "exp"), None, None),
            P(("ctx", "exp"), None, None),
            P("exp", "ctx"),
        ),
        check_vma=False,
    )
```

time: 819 us -> 219 us (0.27); the launches traced: 807 us -> 218 us
  other arithmetic: 433 us -> 4.44 us
  matrix products: 147 us -> 21.8 us
  local copies, waits for them, and re-layouts: 136 us -> 39.7 us
  blocking collectives: 0 us -> 79.2 us
  starting transfers between devices: 59.1 us -> 4.81 us
  Pallas kernels: 0 us -> 26.4 us
  waiting for transfers between devices: 14.4 us -> 27.5 us
    another operation x65 -> x0, other arithmetic: 342 us -> none  [the longest x32 326 us: block_step(): lax.linalg.triangular_solve(system, target, left_side=True, lower=True, u...]
    dot_general x77 -> x5, matrix products: 104 us -> 6.46 us  [the longest x1 2.98 us: body(): grad_gated = jnp.dot(hidden_all, out_proj, preferred_element_type=f32)]
    all_to_all x0 -> x3, blocking collectives: none -> 79.2 us  [the longest x1 35 us: body(): lax.all_to_all(sent, ('ctx', 'exp'), split_axis=0, concat_axis=0, tiled=T...]
    all_to_all x15 -> x1, starting transfers between devices: 58.4 us -> 4.73 us  [body(): lax.all_to_all(y.reshape(ctx_count, tok_rows, columns), 'ctx', split_axis...]
    unnamed x15 -> x0, other arithmetic: 46.7 us -> none
    unnamed x121 -> x56, local copies, waits for them, and re-layouts: 37.3 us -> 9.73 us
    pallas_call x0 -> x2, Pallas kernels: none -> 26.4 us  [the longest x1 13.4 us: delta_forward(): pl.pallas_call(functools.partial(forward_kernel, key_heads, value_heads),...]
    another operation x12 -> x0, matrix products: 25.9 us -> none  [block_step(): lax.linalg.triangular_solve(system, target, left_side=True, lower=True, u...]
  transfers between devices with their start and end apart: 17 -> 3, of which waited for: 6 -> 2; matrix products, arithmetic and copies ran while one was open for 87% -> 16% of each run, Pallas kernels for 0% -> 12%
where the time goes in v1:
time: 219 us; the launch traced here: 218 us
  blocking collectives  79.2 us (36%)
  local copies, waits for them, and re-layouts  39.7 us (18%)
  waiting for transfers between devices  27.5 us (13%)
  Pallas kernels  26.4 us (12%)
  matrix products  21.8 us (10%)
  between operations  14.5 us (7%)
  starting transfers between devices  4.81 us (2%)
  other arithmetic  4.44 us (2%)
    all_to_all x1, blocking collectives, body(): lax.all_to_all(sent, ('ctx', 'exp'), split_axis=0, concat_axis=0, tiled=T...  35 us
    all_to_all x1, blocking collectives, body(): x = lax.all_to_all(outgoing, 'ctx', split_axis=0, concat_axis=0, tiled=True)  25.2 us
    all_to_all x1, blocking collectives, body(): lax.all_to_all(rows_back.reshape(devices, capacity, width), ('ctx', 'exp'...  19.1 us
    all_to_all x1, waiting for transfers between devices, body(): lax.all_to_all(y.reshape(ctx_count, tok_rows, columns), 'ctx', split_axis...  15.9 us
    pallas_call x1, Pallas kernels, delta_forward(): pl.pallas_call(functools.partial(forward_kernel, key_heads, value_heads),...  13.4 us
    pallas_call x1, Pallas kernels, delta_backward(): pl.pallas_call(functools.partial(backward_kernel, key_heads, value_heads)...  13 us
    another operation x10, local copies, waits for them, and re-layouts, by_device(): return tensor[0].reshape(tok_rows, ctx_count, -1)  12 us
    reduce_scatter x1, waiting for transfers between devices, body(): lax.psum_scatter((scale_factor * lax.dot_general(hidden_all, gated_round,...  11.5 us
  transfers between devices with their start and end apart: 3, of which 2 were waited for; matrix products, arithmetic and copies ran while one was open for 16% of the time, Pallas kernels for 12%

profile of v1, /device:TPU:0, one launch (start us, length us, event | category | flops | bytes accessed | tf_op | source)
XLA Modules:
  0.0 218.3 jit_solution(6782082669893984893)
XLA Ops:
  9.2 1.2 fusion.15
  10.4 1.3 fusion.6
  11.8 1.4 convolution_convert_fusion.1
  13.3 1.2 reshape.155
  14.5 35.0 %all_to_all.20 = bf16[32,4,4096]{2,1,0:T(4,128)(2,1)} all-to-all(bf16[32,4,4096]{2,1,0:T(4,128)(2,1)} %reshape.155), channel_id=1, replica_groups=mesh['ctx'=4,'exp'=8] {'ctx','exp'}, dimensions={0} | all-to-all | bytes 2097152 | tf_op jit(solution)/shard_map/all_to_all | solution.py:451
  49.5 1.3 reshape.156
  50.9 3.3 %fusion.2 = f32[128,1024]{1,0:T(8,128)S(1)} fusion(bf16[1,2048,1024]{2,1,0:T(8,128)(2,1)} %param.20, bf16[128,4096]{1,0:T(8,128)(2,1)S(1)} %reshape.156), kind=kOutput, calls=%fused_computation.2 | convolution fusion | flops 536870912 | bytes 5242880 | tf_op jit(solution)/shard_map/dot_general | solution.py:374
  55.2 1.5 copy-done.13
  56.7 1.5 fusion.7
  59.2 19.1 %all_to_all.21 = bf16[32,4,2048]{2,1,0:T(4,128)(2,1)S(1)} all-to-all(bf16[32,4,2048]{2,1,0:T(4,128)(2,1)} %reshape.157), channel_id=1, replica_groups=mesh['ctx'=4,'exp'=8] {'ctx','exp'}, dimensions={0} | all-to-all | bytes 1048576 | tf_op jit(solution)/shard_map/all_to_all | solution.py:460
  80.1 1.5 reshape_squeeze.20
  81.7 2.2 %reshape_squeeze.21 = bf16[128,4,512]{2,1,0:T(4,128)(2,1)} reshape(bf16[1,128,2048]{2,1,0:T(8,128)(2,1)} %param.25) | data formatting | bytes 1048576 | tf_op jit(solution)/shard_map/reshape;squeeze | solution.py:425
  84.0 1.2 copy.77
  87.0 1.8 reshape_squeeze.19
  88.9 1.7 copy.75
  92.8 3.5 %concatenate.12 = bf16[128,4,1664]{2,0,1:T(8,128)(2,1)} concatenate(bf16[128,4,256]{2,0,1:T(8,128)(2,1)S(1)} %copy.74, bf16[128,4,256]{2,0,1:T(8,128)(2,1)} %copy.75, bf16[128,4,512]{2,0,1:T(8,128)(2,1)S(1)} %copy.76, bf16[128,4,512]{2,0,1:T(8,128)(2,1)S(1)} %copy.77, bf16[128,4,4]{2,0,1:T(8,128)(2,1)} %copy.78, bf16[128,4,4]{2,0,1:T(8,128)(2,1)} %copy.79, ...), dimensions={2} | concatenate | bytes 3407872 | tf_op jit(solution)/shard_map/concatenate | solution.py:429
  96.3 25.2 %all_to_all.22 = bf16[4,128,1664]{2,1,0:T(8,128)(2,1)S(1)} all-to-all(bf16[4,128,1664]{2,1,0:T(8,128)(2,1)} %bitcast.87), channel_id=1, replica_groups=mesh['ctx'=4,'exp'=8] {'ctx'}, dimensions={0} | all-to-all | bytes 3407872 | tf_op jit(solution)/shard_map/all_to_all | solution.py:453
  121.5 13.4 %shard_map.222 = (f32[4,4,128,128]{3,2,1,0:T(8,128)S(1)}, f32[4,4,128,128]{3,2,1,0:T(8,128)S(1)}, f32[4,4,128,128]{3,2,1,0:T(8,128)S(1)}, f32[4,4,128,128]{3,2,1,0:T(8,128)S(1)}, bf16[512,512]{1,0:T(8,128)(2,1)S(1)}) custom-call(bf16[512,1664]{1,0:T(8,128)(2,1)S(1)} %bitcast.82, f32[1,128]{1,0:T(1,128)S(1)} %bitcast.85), custom_call_target="tpu_custom_call" | custom-call | flops 9663676416 | bytes 6291456 | tf_op jit(solution)/shard_map/pallas_call | solution.py:320
  134.9 1.2 copy-done.1
  140.0 4.2 %multiply_convert_fusion = bf16[2048,512]{1,0:T(8,128)(2,1)} fusion(bf16[512,2048]{1,0:T(8,128)(2,1)} %all-gather.3.cloned.1.call-done, bf16[512,512]{1,0:T(8,128)(2,1)S(1)} %get-tuple-element.19), kind=kOutput, calls=%fused_computation.4 | convolution fusion | flops 1075838976 | bytes 4718592 | tf_op jit(solution)/shard_map/dot_general | solution.py:479
  144.3 3.0 %fusion.42.grad_ref = f32[512,512]{1,0:T(8,128)S(1)} fusion(bf16[512,2048]{1,0:T(8,128)(2,1)} %all-gather.3.cloned.1.call-done, bf16[2048,512]{1,0:T(8,128)(2,1)S(1)} %copy-done), kind=kOutput, calls=%fused_computation.67 | convolution fusion | flops 1073741824 | bytes 5242880 | tf_op jit(solution)/shard_map/dot_general | solution.py:473
  147.6 13.0 %shard_map.223 = bf16[512,1664]{1,0:T(8,128)(2,1)S(1)} custom-call(bf16[512,1664]{1,0:T(8,128)(2,1)S(1)} %bitcast.83, f32[1,128]{1,0:T(1,128)S(1)} %bitcast.86, f32[4,4,128,128]{3,2,1,0:T(8,128)S(1)} %copy-done.6, f32[4,4,128,128]{3,2,1,0:T(8,128)S(1)} %copy-done.8, f32[4,4,128,128]{3,2,1,0:T(8,128)S(1)} %copy-done.10, f32[4,4,128,128]{3,2,1,0:T(8,128)S(1)} %copy-done.12, ...), custom_call_target="tpu_custom_call" | custom-call | flops 8053063680 | bytes 8388608 | tf_op jit(solution)/shard_map/pallas_call | solution.py:346
  160.6 1.2 copy-done.3
  161.9 4.7 %all-to-all-start.3 = ((bf16[4,128,1664]{2,1,0:T(8,128)(2,1)}), bf16[4,128,1664]{2,1,0:T(8,128)(2,1)}, u32[]{:S(2)}, u32[]{:S(2)}) async-start(bf16[4,128,1664]{2,1,0:T(8,128)(2,1)} %bitcast.84), calls=%async_computation.3 | async-start | bytes 3407872 | tf_op jit(solution)/shard_map/all_to_all | solution.py:487
  166.6 3.3 %convert_bitcast_fusion = bf16[1,2048,1024]{2,1,0:T(8,128)(2,1)} fusion(bf16[128,4096]{1,0:T(8,128)(2,1)S(1)} %copy-done.15, bf16[128,512]{1,0:T(8,128)(2,1)S(1)} %copy-done.21, bf16[128,512]{1,0:T(8,128)(2,1)S(1)} %get-tuple-element.28), kind=kOutput, calls=%fused_computation.5 | convolution fusion | flops 539492352 | bytes 4980736 | tf_op jit(solution)/shard_map/dot_general | solution.py:389
  169.9 2.1 fusion.4
  172.0 15.9 %all-to-all-done.3 = bf16[4,128,1664]{2,1,0:T(8,128)(2,1)} async-done(((bf16[4,128,1664]{2,1,0:T(8,128)(2,1)}), bf16[4,128,1664]{2,1,0:T(8,128)(2,1)}, u32[]{:S(2)}, u32[]{:S(2)}) %all-to-all-start.3) | async-done | bytes 1703968 | tf_op jit(solution)/shard_map/all_to_all | solution.py:487
  187.9 1.3 slice_bitcast_fusion
  189.7 1.2 reshape.162
  191.2 1.2 reshape.163
  198.1 11.5 %reduce-scatter.2.cloned.1.call-done = bf16[256,512]{1,0:T(8,128)(2,1)} async-done(((bf16[2048,512]{1,0:T(8,128)(2,1)}), bf16[256,512]{1,0:T(8,128)(2,1)}) %reduce-scatter.2.cloned.1.call-update) | async-done | bytes 262160 | tf_op jit(solution)/shard_map/reduce_scatter | solution.py:476
  209.7 1.8 convert_element_type.63
  (86 shorter events, 20.8 us)
Async XLA Ops:
  7.2 137.1 %copy-start = (bf16[2048,512]{1,0:T(8,128)(2,1)S(1)}, bf16[2048,512]{1,0:T(8,128)(2,1)}, u32[]{:S(2)}) copy-start(bf16[2048,512]{1,0:T(8,128)(2,1)} %param.29) | copy-start | bytes 6291460
  7.2 132.9 %all-gather.3.cloned.1.call-start = ((), (), s32[]{:S(2)}) async-start(), calls=%async_computation.6 | async-start | bytes 2621440 | tf_op jit(solution)/shard_map/all_gather | solution.py:472
  50.9 3.3 %copy-start.14 = (bf16[128,4096]{1,0:T(8,128)(2,1)}, bf16[128,4096]{1,0:T(8,128)(2,1)S(1)}, u32[]{:S(2)}) copy-start(bf16[128,4096]{1,0:T(8,128)(2,1)S(1)} %reshape.156) | copy-start | bytes 3145732
  50.9 3.3 %copy-start.26 = (bf16[1,512,2048]{2,1,0:T(8,128)(2,1)S(1)}, bf16[1,512,2048]{2,1,0:T(8,128)(2,1)}, u32[]{:S(2)}) copy-start(bf16[1,512,2048]{2,1,0:T(8,128)(2,1)} %param.21) | copy-start | bytes 6291460
  54.2 0.9 copy-start.18
  54.2 2.4 %copy-start.13 = (bf16[1,2048,1024]{2,1,0:T(8,128)(2,1)S(1)}, bf16[1,2048,1024]{2,1,0:T(8,128)(2,1)}, u32[]{:S(2)}) copy-start(bf16[1,2048,1024]{2,1,0:T(8,128)(2,1)} %param.20) | copy-start | bytes 12582916
  55.1 3.1 %copy-start.20 = (bf16[128,512]{1,0:T(8,128)(2,1)}, bf16[128,512]{1,0:T(8,128)(2,1)S(1)}, u32[]{:S(2)}) copy-start(bf16[128,512]{1,0:T(8,128)(2,1)S(1)} %get-tuple-element.29) | copy-start | bytes 393220
  58.2 20.1 %copy-start.16 = (bf16[1,128,2048]{2,1,0:T(8,128)(2,1)S(1)}, bf16[1,128,2048]{2,1,0:T(8,128)(2,1)}, u32[]{:S(2)}) copy-start(bf16[1,128,2048]{2,1,0:T(8,128)(2,1)} %param.15) | copy-start | bytes 1572868
  58.2 20.1 %copy-start.23 = (f32[2048]{0:T(1024)S(1)}, f32[2048]{0:T(1024)}, u32[]{:S(2)}) copy-start(f32[2048]{0:T(1024)} %param.17) | copy-start | bytes 24580
  59.2 19.7 %copy-start.17 = (bf16[1,128,2048]{2,1,0:T(8,128)(2,1)S(1)}, bf16[1,128,2048]{2,1,0:T(8,128)(2,1)}, u32[]{:S(2)}) copy-start(bf16[1,128,2048]{2,1,0:T(8,128)(2,1)} %param.16) | copy-start | bytes 1572868
  80.1 5.1 %copy-start.22 = (bf16[1,128,1024]{2,1,0:T(8,128)(2,1)S(1)}, bf16[1,128,1024]{2,1,0:T(8,128)(2,1)}, u32[]{:S(2)}) copy-start(bf16[1,128,1024]{2,1,0:T(8,128)(2,1)} %param.22) | copy-start | bytes 786436
  80.1 129.6 %reduce-scatter.2.cloned.1.call-start = ((), (), s32[]{:S(2)}) async-start(), calls=%async_computation.5 | async-start | bytes 2359296 | tf_op jit(solution)/shard_map/reduce_scatter | solution.py:476
  81.7 8.8 %copy-start.24 = (bf16[1,128,16]{1,2,0:T(8,128)(2,1)S(1)}, bf16[1,128,16]{1,2,0:T(8,128)(2,1)}, u32[]{:S(2)}) copy-start(bf16[1,128,16]{1,2,0:T(8,128)(2,1)} %param.26) | copy-start | bytes 12292
  81.7 9.6 %copy-start.25 = (bf16[1,128,16]{1,2,0:T(8,128)(2,1)S(1)}, bf16[1,128,16]{1,2,0:T(8,128)(2,1)}, u32[]{:S(2)}) copy-start(bf16[1,128,16]{1,2,0:T(8,128)(2,1)} %param.27) | copy-start | bytes 12292
  96.3 25.2 %copy-start.4 = (f32[128]{0:T(128)S(1)}, f32[128]{0:T(128)}, u32[]{:S(2)}) copy-start(f32[128]{0:T(128)} %param.28) | copy-start | bytes 1540
  134.9 1.2 copy-start.1
  136.1 1.0 copy-start.5
  137.1 1.0 copy-start.7
  138.0 1.0 copy-start.9
  139.0 1.0 copy-start.11
  144.3 3.0 %copy-start.2 = (bf16[4,128,1664]{2,1,0:T(8,128)(2,1)S(1)}, bf16[4,128,1664]{2,1,0:T(8,128)(2,1)}, u32[]{:S(2)}) copy-start(bf16[4,128,1664]{2,1,0:T(8,128)(2,1)} %copy-done.1) | copy-start | bytes 5111812
  144.3 3.0 %copy-start.6 = (f32[4,4,128,128]{3,2,1,0:T(8,128)S(1)}, f32[4,4,128,128]{3,2,1,0:T(8,128)}, u32[]{:S(2)}) copy-start(f32[4,4,128,128]{3,2,1,0:T(8,128)} %copy-done.5) | copy-start | bytes 3145732
  144.3 3.0 %copy-start.8 = (f32[4,4,128,128]{3,2,1,0:T(8,128)S(1)}, f32[4,4,128,128]{3,2,1,0:T(8,128)}, u32[]{:S(2)}) copy-start(f32[4,4,128,128]{3,2,1,0:T(8,128)} %copy-done.7) | copy-start | bytes 3145732
  144.3 3.0 %copy-start.10 = (f32[4,4,128,128]{3,2,1,0:T(8,128)S(1)}, f32[4,4,128,128]{3,2,1,0:T(8,128)}, u32[]{:S(2)}) copy-start(f32[4,4,128,128]{3,2,1,0:T(8,128)} %copy-done.9) | copy-start | bytes 3145732
  144.3 3.3 %copy-start.12 = (f32[4,4,128,128]{3,2,1,0:T(8,128)S(1)}, f32[4,4,128,128]{3,2,1,0:T(8,128)}, u32[]{:S(2)}) copy-start(f32[4,4,128,128]{3,2,1,0:T(8,128)} %copy-done.11) | copy-start | bytes 3145732
  160.6 1.2 copy-start.3
  161.9 4.7 %copy-start.15 = (bf16[128,4096]{1,0:T(8,128)(2,1)S(1)}, bf16[128,4096]{1,0:T(8,128)(2,1)}, u32[]{:S(2)}) copy-start(bf16[128,4096]{1,0:T(8,128)(2,1)} %copy-done.14) | copy-start | bytes 3145732
  161.9 4.7 %copy-start.21 = (bf16[128,512]{1,0:T(8,128)(2,1)S(1)}, bf16[128,512]{1,0:T(8,128)(2,1)}, u32[]{:S(2)}) copy-start(bf16[128,512]{1,0:T(8,128)(2,1)} %copy-done.20) | copy-start | bytes 393220
  161.9 26.1 %all-to-all-start.3 = ((bf16[4,128,1664]{2,1,0:T(8,128)(2,1)}), bf16[4,128,1664]{2,1,0:T(8,128)(2,1)}, u32[]{:S(2)}, u32[]{:S(2)}) async-start(bf16[4,128,1664]{2,1,0:T(8,128)(2,1)} %bitcast.84), calls=%async_computation.3 | async-start | bytes 3407872 | tf_op jit(solution)/shard_map/all_to_all | solution.py:487
  166.6 3.3 %copy-start.19 = (f32[128,1024]{1,0:T(8,128)S(1)}, f32[128,1024]{1,0:T(8,128)}, u32[]{:S(2)}) copy-start(f32[128,1024]{1,0:T(8,128)} %copy-done.18) | copy-start | bytes 1572868
Sparse Core Ops, SparseCore 0:
  80.2 20.1 all-gather.2
  144.4 65.2 reduce-scatter.1

commit v2 on v1

--- a/solution.py
+++ b/solution.py
@@ -421,13 +421,13 @@
     value_heads = value_in.shape[2] // LANES // ctx_count
     slots = devices * capacity
 
-    def by_device(tensor):
-        return tensor[0].reshape(tok_rows, ctx_count, -1)
-
-    packed = [by_device(t) for t in (query_in, key_in, value_in, gate_in, decay_logit, beta_logit)]
-    packed.append(jnp.zeros((tok_rows, ctx_count, LANES - 2 * value_heads), bf16))
-    outgoing = jnp.concatenate(packed, axis=2).transpose(1, 0, 2)
-    columns = outgoing.shape[2]
+    received = [
+        lax.all_to_all(t, "ctx", split_axis=2, concat_axis=1, tiled=True)[0]
+        for t in (query_in, key_in, value_in, gate_in, decay_logit, beta_logit)
+    ]
+    received.append(jnp.zeros((ctx_count * tok_rows, LANES - 2 * value_heads), bf16))
+    x = jnp.concatenate(received, axis=1)
+    columns = x.shape[1]
 
     flat_hidden = hidden_in[0].astype(f32)
     normed, norm_back = jax.vjp(lambda tensor: post_norm(tensor, post_gain), flat_hidden)
@@ -450,8 +450,6 @@
     sent = jnp.concatenate([rows_in, rows_grad], axis=1).reshape(devices, capacity, 2 * width)
     got = lax.all_to_all(sent, ("ctx", "exp"), split_axis=0, concat_axis=0, tiled=True)
     got = got.reshape(slots, 2 * width)
-    x = lax.all_to_all(outgoing, "ctx", split_axis=0, concat_axis=0, tiled=True)
-    x = x.reshape(ctx_count * tok_rows, columns)
     gain = head_gain[None, :]
     *kept, gated_round = delta_forward(x, gain, key_heads, value_heads)
     rows_back, grad_gate_up, grad_down = expert_backward(

time: 219 us -> 269 us (1.23)
  other arithmetic: 4.44 us -> 34.9 us
  blocking collectives: 79.2 us -> 54.1 us
  starting transfers between devices: 4.81 us -> 27.5 us
  local copies, waits for them, and re-layouts: 39.7 us -> 53.9 us
  waiting for transfers between devices: 27.5 us -> 34.2 us
    unnamed x0 -> x6, other arithmetic: none -> 30.4 us
    all_to_all x1 -> x0, blocking collectives: 25.2 us -> none  [body(): x = lax.all_to_all(outgoing, 'ctx', split_axis=0, concat_axis=0, tiled=True)]
    all_to_all x0 -> x6, starting transfers between devices: none -> 22.4 us  [body(): lax.all_to_all(t, 'ctx', split_axis=2, concat_axis=1, tiled=True)[0]]
    unnamed x56 -> x83, local copies, waits for them, and re-layouts: 9.73 us -> 30.5 us
    another operation x10 -> x0, local copies, waits for them, and re-layouts: 12 us -> none  [by_device(): return tensor[0].reshape(tok_rows, ctx_count, -1)]
    all_to_all x0 -> x6, local copies, waits for them, and re-layouts: none -> 5.92 us  [body(): lax.all_to_all(t, 'ctx', split_axis=2, concat_axis=1, tiled=True)[0]]
    all_to_all x0 -> x6, waiting for transfers between devices: none -> 5.4 us  [body(): lax.all_to_all(t, 'ctx', split_axis=2, concat_axis=1, tiled=True)[0]]
  transfers between devices with their start and end apart: 3 -> 9, of which waited for: 2 -> 5; matrix products, arithmetic and copies ran while one was open for 16% -> 30% of each run, Pallas kernels for 12% -> 10%
where the time goes in v2:
time: 269 us; the launch traced here: 267 us
  blocking collectives  54.1 us (20%)
  local copies, waits for them, and re-layouts  53.9 us (20%)
  other arithmetic  34.9 us (13%)
  waiting for transfers between devices  34.2 us (13%)
  starting transfers between devices  27.5 us (10%)
  Pallas kernels  26.4 us (10%)
  matrix products  21.8 us (8%)
  between operations  14.7 us (5%)
    all_to_all x1, blocking collectives, body(): lax.all_to_all(sent, ('ctx', 'exp'), split_axis=0, concat_axis=0, tiled=T...  35 us
    unnamed x83, local copies, waits for them, and re-layouts  30.5 us
    unnamed x6, other arithmetic  30.4 us
    all_to_all x6, starting transfers between devices, body(): lax.all_to_all(t, 'ctx', split_axis=2, concat_axis=1, tiled=True)[0]  22.4 us
    all_to_all x1, blocking collectives, body(): lax.all_to_all(rows_back.reshape(devices, capacity, width), ('ctx', 'exp'...  19.1 us
    all_to_all x1, waiting for transfers between devices, body(): lax.all_to_all(y.reshape(ctx_count, tok_rows, columns), 'ctx', split_axis...  16.1 us
    pallas_call x1, Pallas kernels, delta_forward(): pl.pallas_call(functools.partial(forward_kernel, key_heads, value_heads),...  13.4 us
    pallas_call x1, Pallas kernels, delta_backward(): pl.pallas_call(functools.partial(backward_kernel, key_heads, value_heads)...  13 us
  transfers between devices with their start and end apart: 9, of which 5 were waited for; matrix products, arithmetic and copies ran while one was open for 30% of the time, Pallas kernels for 10%

profile of v2, /device:TPU:0, one launch (start us, length us, event | category | flops | bytes accessed | tf_op | source)
XLA Modules:
  0.0 267.4 jit_solution(5848955515721710230)
XLA Ops:
  14.5 35.0 %all_to_all.105 = bf16[32,4,4096]{2,1,0:T(4,128)(2,1)} all-to-all(bf16[32,4,4096]{2,1,0:T(4,128)(2,1)} %reshape.158), channel_id=1, replica_groups=mesh['ctx'=4,'exp'=8] {'ctx','exp'}, dimensions={0} | all-to-all | bytes 2097152 | tf_op jit(solution)/shard_map/all_to_all | solution.py:451
  50.9 3.3 %fusion.2 = f32[128,1024]{1,0:T(8,128)S(1)} fusion(bf16[1,2048,1024]{2,1,0:T(8,128)(2,1)} %param.20, bf16[128,4096]{1,0:T(8,128)(2,1)S(1)} %reshape.159), kind=kOutput, calls=%fused_computation.2 | convolution fusion | flops 536870912 | bytes 5242880 | tf_op jit(solution)/shard_map/dot_general | solution.py:374
  59.2 19.1 %all_to_all.106 = bf16[32,4,2048]{2,1,0:T(4,128)(2,1)S(1)} all-to-all(bf16[32,4,2048]{2,1,0:T(4,128)(2,1)} %reshape.160), channel_id=1, replica_groups=mesh['ctx'=4,'exp'=8] {'ctx','exp'}, dimensions={0} | all-to-all | bytes 1048576 | tf_op jit(solution)/shard_map/all_to_all | solution.py:458
  81.9 3.3 %all-to-all-start.6 = ((bf16[4,2,256]{2,1,0:T(2,128)(2,1)}), bf16[4,2,256]{2,1,0:T(2,128)(2,1)S(1)}, u32[]{:S(2)}, u32[]{:S(2)}) async-start(bf16[4,2,256]{2,1,0:T(2,128)(2,1)} %reshape.180), calls=%async_computation.6 | async-start | bytes 8192 | tf_op jit(solution)/shard_map/all_to_all | solution.py:425
  86.5 2.4 all-to-all-done.6
  89.0 3.2 %all-to-all-start.7 = ((bf16[4,2,256]{2,1,0:T(2,128)(2,1)}), bf16[4,2,256]{2,1,0:T(2,128)(2,1)S(1)}, u32[]{:S(2)}, u32[]{:S(2)}) async-start(bf16[4,2,256]{2,1,0:T(2,128)(2,1)} %reshape.182), calls=%async_computation.7 | async-start | bytes 8192 | tf_op jit(solution)/shard_map/all_to_all | solution.py:425
  92.6 2.2 reduce
  96.0 3.4 %all-to-all-start.2 = ((bf16[4,2,16384]{2,1,0:T(2,128)(2,1)}), bf16[4,2,16384]{2,1,0:T(2,128)(2,1)S(1)}, u32[]{:S(2)}, u32[]{:S(2)}) async-start(bf16[4,2,16384]{2,1,0:T(2,128)(2,1)} %reshape.172), calls=%async_computation.2 | async-start | bytes 524288 | tf_op jit(solution)/shard_map/all_to_all | solution.py:425
  99.8 2.2 reduce.1
  102.8 2.6 all-to-all-done.2
  105.4 4.2 %all-to-all-start.3 = ((bf16[4,2,16384]{2,1,0:T(2,128)(2,1)}), bf16[4,2,16384]{2,1,0:T(2,128)(2,1)}, u32[]{:S(2)}, u32[]{:S(2)}) async-start(bf16[4,2,16384]{2,1,0:T(2,128)(2,1)} %reshape.174), calls=%async_computation.3 | async-start | bytes 524288 | tf_op jit(solution)/shard_map/all_to_all | solution.py:425
  109.6 2.4 copy.106
  112.0 12.3 %reduce.2 = bf16[2048,128]{1,0:T(8,128)(2,1)} reduce(bf16[2048,1,128]{2,1,0:T(2,128)(2,1)S(1)} %bitcast.124, bf16[]{:T(256)} %broadcast.99), dimensions={1}, to_apply=%bitcast.95.reduce_sub_computation | reduce | bytes 1048578
  124.3 2.0 reshape.176
  126.3 4.1 %all-to-all-start.4 = ((bf16[4,2,32768]{2,1,0:T(2,128)(2,1)}), bf16[4,2,32768]{2,1,0:T(2,128)(2,1)}, u32[]{:S(2)}, u32[]{:S(2)}) async-start(bf16[4,2,32768]{2,1,0:T(2,128)(2,1)} %reshape.176), calls=%async_computation.4 | async-start | bytes 1048576 | tf_op jit(solution)/shard_map/all_to_all | solution.py:425
  130.4 2.4 copy.108
  132.8 12.3 %reduce.3 = bf16[2048,128]{1,0:T(8,128)(2,1)} reduce(bf16[2048,1,128]{2,1,0:T(2,128)(2,1)S(1)} %bitcast.123, bf16[]{:T(256)} %broadcast.99), dimensions={1}, to_apply=%bitcast.97.reduce_sub_computation | reduce | bytes 1048578
  145.1 2.0 reshape.178
  147.1 4.1 %all-to-all-start.5 = ((bf16[4,2,32768]{2,1,0:T(2,128)(2,1)}), bf16[4,2,32768]{2,1,0:T(2,128)(2,1)}, u32[]{:S(2)}, u32[]{:S(2)}) async-start(bf16[4,2,32768]{2,1,0:T(2,128)(2,1)} %reshape.178), calls=%async_computation.5 | async-start | bytes 1048576 | tf_op jit(solution)/shard_map/all_to_all | solution.py:425
  155.7 2.2 reshape.177
  158.8 2.0 copy.107
  160.8 2.2 reshape.179
  165.2 3.6 %concatenate.12.x_ref = bf16[512,1664]{1,0:T(8,128)(2,1)} concatenate(bf16[512,256]{1,0:T(8,128)(2,1)S(1)} %bitcast.134, bf16[512,256]{1,0:T(8,128)(2,1)} %bitcast.135, bf16[512,512]{1,0:T(8,128)(2,1)} %bitcast.126, bf16[512,512]{1,0:T(8,128)(2,1)S(1)} %bitcast.127, bf16[512,4]{1,0:T(8,128)(2,1)} %bitcast.138, bf16[512,4]{1,0:T(8,128)(2,1)} %bitcast.139, ...), dimensions={1} | concatenate | bytes 3407872 | tf_op jit(solution)/shard_map/concatenate | solution.py:429
  170.2 13.4 %shard_map.222 = (f32[4,4,128,128]{3,2,1,0:T(8,128)S(1)}, f32[4,4,128,128]{3,2,1,0:T(8,128)S(1)}, f32[4,4,128,128]{3,2,1,0:T(8,128)S(1)}, f32[4,4,128,128]{3,2,1,0:T(8,128)S(1)}, bf16[512,512]{1,0:T(8,128)(2,1)S(1)}) custom-call(bf16[512,1664]{1,0:T(8,128)(2,1)S(1)} %copy-done.1, f32[1,128]{1,0:T(1,128)S(1)} %bitcast.119), custom_call_target="tpu_custom_call" | custom-call | flops 9663676416 | bytes 6291456 | tf_op jit(solution)/shard_map/pallas_call | solution.py:320
  187.7 4.2 %multiply_convert_fusion = bf16[2048,512]{1,0:T(8,128)(2,1)} fusion(bf16[512,2048]{1,0:T(8,128)(2,1)} %all-gather.3.cloned.1.call-done, bf16[512,512]{1,0:T(8,128)(2,1)S(1)} %get-tuple-element.19), kind=kOutput, calls=%fused_computation.4 | convolution fusion | flops 1075838976 | bytes 4718592 | tf_op jit(solution)/shard_map/dot_general | solution.py:477
  192.0 3.0 %fusion.42.grad_ref = f32[512,512]{1,0:T(8,128)S(1)} fusion(bf16[512,2048]{1,0:T(8,128)(2,1)} %all-gather.3.cloned.1.call-done, bf16[2048,512]{1,0:T(8,128)(2,1)S(1)} %copy-done), kind=kOutput, calls=%fused_computation.69 | convolution fusion | flops 1073741824 | bytes 5242880 | tf_op jit(solution)/shard_map/dot_general | solution.py:471
  195.2 13.0 %shard_map.223 = bf16[512,1664]{1,0:T(8,128)(2,1)S(1)} custom-call(bf16[512,1664]{1,0:T(8,128)(2,1)S(1)} %copy-done.2, f32[1,128]{1,0:T(1,128)S(1)} %bitcast.120, f32[4,4,128,128]{3,2,1,0:T(8,128)S(1)} %copy-done.6, f32[4,4,128,128]{3,2,1,0:T(8,128)S(1)} %copy-done.8, f32[4,4,128,128]{3,2,1,0:T(8,128)S(1)} %copy-done.10, f32[4,4,128,128]{3,2,1,0:T(8,128)S(1)} %copy-done.12, ...), custom_call_target="tpu_custom_call" | custom-call | flops 8053063680 | bytes 8388608 | tf_op jit(solution)/shard_map/pallas_call | solution.py:346
  209.5 4.8 %all-to-all-start.8 = ((bf16[4,128,1664]{2,1,0:T(8,128)(2,1)}), bf16[4,128,1664]{2,1,0:T(8,128)(2,1)}, u32[]{:S(2)}, u32[]{:S(2)}) async-start(bf16[4,128,1664]{2,1,0:T(8,128)(2,1)} %bitcast.118), calls=%async_computation.8 | async-start | bytes 3407872 | tf_op jit(solution)/shard_map/all_to_all | solution.py:485
  214.3 3.3 %convert_bitcast_fusion = bf16[1,2048,1024]{2,1,0:T(8,128)(2,1)} fusion(bf16[128,4096]{1,0:T(8,128)(2,1)S(1)} %copy-done.15, bf16[128,512]{1,0:T(8,128)(2,1)S(1)} %copy-done.21, bf16[128,512]{1,0:T(8,128)(2,1)S(1)} %get-tuple-element.28), kind=kOutput, calls=%fused_computation.5 | convolution fusion | flops 539492352 | bytes 4980736 | tf_op jit(solution)/shard_map/dot_general | solution.py:389
  217.6 2.1 fusion.4
  219.7 16.1 %all-to-all-done.8 = bf16[4,128,1664]{2,1,0:T(8,128)(2,1)} async-done(((bf16[4,128,1664]{2,1,0:T(8,128)(2,1)}), bf16[4,128,1664]{2,1,0:T(8,128)(2,1)}, u32[]{:S(2)}, u32[]{:S(2)}) %all-to-all-start.8) | async-done | bytes 1703968 | tf_op jit(solution)/shard_map/all_to_all | solution.py:485
  246.1 12.7 %reduce-scatter.2.cloned.1.call-done = bf16[256,512]{1,0:T(8,128)(2,1)} async-done(((bf16[2048,512]{1,0:T(8,128)(2,1)}), bf16[256,512]{1,0:T(8,128)(2,1)}) %reduce-scatter.2.cloned.1.call-update) | async-done | bytes 262160 | tf_op jit(solution)/shard_map/reduce_scatter | solution.py:474
  (126 shorter events, 47.6 us)
Async XLA Ops:
  7.2 184.7 %copy-start = (bf16[2048,512]{1,0:T(8,128)(2,1)S(1)}, bf16[2048,512]{1,0:T(8,128)(2,1)}, u32[]{:S(2)}) copy-start(bf16[2048,512]{1,0:T(8,128)(2,1)} %param.29) | copy-start | bytes 6291460
  7.2 180.5 %all-gather.3.cloned.1.call-start = ((), (), s32[]{:S(2)}) async-start(), calls=%async_computation.11 | async-start | bytes 2621440 | tf_op jit(solution)/shard_map/all_gather | solution.py:470
  50.9 3.3 %copy-start.14 = (bf16[128,4096]{1,0:T(8,128)(2,1)}, bf16[128,4096]{1,0:T(8,128)(2,1)S(1)}, u32[]{:S(2)}) copy-start(bf16[128,4096]{1,0:T(8,128)(2,1)S(1)} %reshape.159) | copy-start | bytes 3145732
  50.9 3.3 %copy-start.27 = (bf16[1,512,2048]{2,1,0:T(8,128)(2,1)S(1)}, bf16[1,512,2048]{2,1,0:T(8,128)(2,1)}, u32[]{:S(2)}) copy-start(bf16[1,512,2048]{2,1,0:T(8,128)(2,1)} %param.21) | copy-start | bytes 6291460
  54.2 2.4 copy-start.13
  55.1 3.1 %copy-start.20 = (bf16[128,512]{1,0:T(8,128)(2,1)}, bf16[128,512]{1,0:T(8,128)(2,1)S(1)}, u32[]{:S(2)}) copy-start(bf16[128,512]{1,0:T(8,128)(2,1)S(1)} %get-tuple-element.29) | copy-start | bytes 393220
  58.2 20.1 %copy-start.16 = (bf16[1,128,2048]{2,1,0:T(8,128)(2,1)S(1)}, bf16[1,128,2048]{2,1,0:T(8,128)(2,1)}, u32[]{:S(2)}) copy-start(bf16[1,128,2048]{2,1,0:T(8,128)(2,1)} %param.15) | copy-start | bytes 1572868
  58.2 20.1 %copy-start.24 = (f32[2048]{0:T(1024)S(1)}, f32[2048]{0:T(1024)}, u32[]{:S(2)}) copy-start(f32[2048]{0:T(1024)} %param.17) | copy-start | bytes 24580
  59.2 19.7 %copy-start.17 = (bf16[1,128,2048]{2,1,0:T(8,128)(2,1)S(1)}, bf16[1,128,2048]{2,1,0:T(8,128)(2,1)}, u32[]{:S(2)}) copy-start(bf16[1,128,2048]{2,1,0:T(8,128)(2,1)} %param.16) | copy-start | bytes 1572868
  78.9 1.2 copy-start.25
  78.9 6.3 %copy-start.26 = (bf16[1,128,16]{1,2,0:T(8,128)(2,1)S(1)}, bf16[1,128,16]{1,2,0:T(8,128)(2,1)}, u32[]{:S(2)}) copy-start(bf16[1,128,16]{1,2,0:T(8,128)(2,1)} %param.27) | copy-start | bytes 12292
  78.9 13.3 %copy-start.22 = (bf16[1,128,1024]{2,1,0:T(8,128)(2,1)S(1)}, bf16[1,128,1024]{2,1,0:T(8,128)(2,1)}, u32[]{:S(2)}) copy-start(bf16[1,128,1024]{2,1,0:T(8,128)(2,1)} %param.22) | copy-start | bytes 786436
  80.1 19.3 %copy-start.23 = (bf16[1,128,1024]{2,1,0:T(8,128)(2,1)S(1)}, bf16[1,128,1024]{2,1,0:T(8,128)(2,1)}, u32[]{:S(2)}) copy-start(bf16[1,128,1024]{2,1,0:T(8,128)(2,1)} %param.23) | copy-start | bytes 786436
  81.9 7.0 %all-to-all-start.6 = ((bf16[4,2,256]{2,1,0:T(2,128)(2,1)}), bf16[4,2,256]{2,1,0:T(2,128)(2,1)S(1)}, u32[]{:S(2)}, u32[]{:S(2)}) async-start(bf16[4,2,256]{2,1,0:T(2,128)(2,1)} %reshape.180), calls=%async_computation.6 | async-start | bytes 8192 | tf_op jit(solution)/shard_map/all_to_all | solution.py:425
  89.0 7.0 %all-to-all-start.7 = ((bf16[4,2,256]{2,1,0:T(2,128)(2,1)}), bf16[4,2,256]{2,1,0:T(2,128)(2,1)S(1)}, u32[]{:S(2)}, u32[]{:S(2)}) async-start(bf16[4,2,256]{2,1,0:T(2,128)(2,1)} %reshape.182), calls=%async_computation.7 | async-start | bytes 8192 | tf_op jit(solution)/shard_map/all_to_all | solution.py:425
  96.0 9.4 %all-to-all-start.2 = ((bf16[4,2,16384]{2,1,0:T(2,128)(2,1)}), bf16[4,2,16384]{2,1,0:T(2,128)(2,1)S(1)}, u32[]{:S(2)}, u32[]{:S(2)}) async-start(bf16[4,2,16384]{2,1,0:T(2,128)(2,1)} %reshape.172), calls=%async_computation.2 | async-start | bytes 524288 | tf_op jit(solution)/shard_map/all_to_all | solution.py:425
  105.4 20.9 %all-to-all-start.3 = ((bf16[4,2,16384]{2,1,0:T(2,128)(2,1)}), bf16[4,2,16384]{2,1,0:T(2,128)(2,1)}, u32[]{:S(2)}, u32[]{:S(2)}) async-start(bf16[4,2,16384]{2,1,0:T(2,128)(2,1)} %reshape.174), calls=%async_computation.3 | async-start | bytes 524288 | tf_op jit(solution)/shard_map/all_to_all | solution.py:425
  126.3 20.8 %all-to-all-start.4 = ((bf16[4,2,32768]{2,1,0:T(2,128)(2,1)}), bf16[4,2,32768]{2,1,0:T(2,128)(2,1)}, u32[]{:S(2)}, u32[]{:S(2)}) async-start(bf16[4,2,32768]{2,1,0:T(2,128)(2,1)} %reshape.176), calls=%async_computation.4 | async-start | bytes 1048576 | tf_op jit(solution)/shard_map/all_to_all | solution.py:425
  147.1 13.8 %all-to-all-start.5 = ((bf16[4,2,32768]{2,1,0:T(2,128)(2,1)}), bf16[4,2,32768]{2,1,0:T(2,128)(2,1)}, u32[]{:S(2)}, u32[]{:S(2)}) async-start(bf16[4,2,32768]{2,1,0:T(2,128)(2,1)} %reshape.178), calls=%async_computation.5 | async-start | bytes 1048576 | tf_op jit(solution)/shard_map/all_to_all | solution.py:425
  151.2 107.5 %reduce-scatter.2.cloned.1.call-start = ((), (), s32[]{:S(2)}) async-start(), calls=%async_computation.10 | async-start | bytes 2359296 | tf_op jit(solution)/shard_map/reduce_scatter | solution.py:474
  165.2 3.6 %copy-start.4 = (f32[128]{0:T(128)S(1)}, f32[128]{0:T(128)}, u32[]{:S(2)}) copy-start(f32[128]{0:T(128)} %param.28) | copy-start | bytes 1540
  168.8 1.5 copy-start.1
  191.9 3.0 %copy-start.2 = (bf16[512,1664]{1,0:T(8,128)(2,1)S(1)}, bf16[512,1664]{1,0:T(8,128)(2,1)}, u32[]{:S(2)}) copy-start(bf16[512,1664]{1,0:T(8,128)(2,1)} %concatenate.12.x_ref) | copy-start | bytes 5111812
  191.9 3.0 %copy-start.6 = (f32[4,4,128,128]{3,2,1,0:T(8,128)S(1)}, f32[4,4,128,128]{3,2,1,0:T(8,128)}, u32[]{:S(2)}) copy-start(f32[4,4,128,128]{3,2,1,0:T(8,128)} %copy-done.5) | copy-start | bytes 3145732
  191.9 3.0 %copy-start.8 = (f32[4,4,128,128]{3,2,1,0:T(8,128)S(1)}, f32[4,4,128,128]{3,2,1,0:T(8,128)}, u32[]{:S(2)}) copy-start(f32[4,4,128,128]{3,2,1,0:T(8,128)} %copy-done.7) | copy-start | bytes 3145732
  191.9 3.0 %copy-start.10 = (f32[4,4,128,128]{3,2,1,0:T(8,128)S(1)}, f32[4,4,128,128]{3,2,1,0:T(8,128)}, u32[]{:S(2)}) copy-start(f32[4,4,128,128]{3,2,1,0:T(8,128)} %copy-done.9) | copy-start | bytes 3145732
  191.9 3.3 %copy-start.12 = (f32[4,4,128,128]{3,2,1,0:T(8,128)S(1)}, f32[4,4,128,128]{3,2,1,0:T(8,128)}, u32[]{:S(2)}) copy-start(f32[4,4,128,128]{3,2,1,0:T(8,128)} %copy-done.11) | copy-start | bytes 3145732
  208.2 1.2 copy-start.3
  209.5 4.8 %copy-start.15 = (bf16[128,4096]{1,0:T(8,128)(2,1)S(1)}, bf16[128,4096]{1,0:T(8,128)(2,1)}, u32[]{:S(2)}) copy-start(bf16[128,4096]{1,0:T(8,128)(2,1)} %copy-done.14) | copy-start | bytes 3145732
  209.5 4.8 %copy-start.21 = (bf16[128,512]{1,0:T(8,128)(2,1)S(1)}, bf16[128,512]{1,0:T(8,128)(2,1)}, u32[]{:S(2)}) copy-start(bf16[128,512]{1,0:T(8,128)(2,1)} %copy-done.20) | copy-start | bytes 393220
  209.5 26.3 %all-to-all-start.8 = ((bf16[4,128,1664]{2,1,0:T(8,128)(2,1)}), bf16[4,128,1664]{2,1,0:T(8,128)(2,1)}, u32[]{:S(2)}, u32[]{:S(2)}) async-start(bf16[4,128,1664]{2,1,0:T(8,128)(2,1)} %bitcast.118), calls=%async_computation.8 | async-start | bytes 3407872 | tf_op jit(solution)/shard_map/all_to_all | solution.py:485
  214.3 3.3 %copy-start.19 = (f32[128,1024]{1,0:T(8,128)S(1)}, f32[128,1024]{1,0:T(8,128)}, u32[]{:S(2)}) copy-start(f32[128,1024]{1,0:T(8,128)} %copy-done.18) | copy-start | bytes 1572868
  (5 other events, 5.0 us)
Sparse Core Ops, SparseCore 0:
  80.2 20.2 all-gather.2
  192.0 66.6 reduce-scatter.1
